TPU v7x, 256 devices: a whole 4x4x8 slice. The times are simulated.
256 devices in a mesh: tm: 8 (over z), row: 4 (over x), col: 8 (over y, core).
Axes of the slice: x: 4, y: 4, z: 8, core: 2. Of those that a mesh axis runs over, the one named last changes fastest.
Arguments:
- activations: bfloat16 [32, 64, 128, 256], P('tm', 'row', 'col'), may hold values from -300 to 300
- cotangent: bfloat16 [32, 64, 128, 256], P('tm', 'row', 'col'), may hold values from -80 to 80
- conv_first: bfloat16 [3, 3, 3, 256, 256], replicated, may hold values from -0.078125 to 0.078125
- bias_first: float32 [256], replicated, may hold values from -4 to 4
- gain_first: float32 [256], replicated, may hold values from 0.1 to 1.9
- offset_first: float32 [256], replicated, may hold values from -4 to 4
- conv_second: bfloat16 [3, 3, 3, 256, 256], replicated, may hold values from -0.078125 to 0.078125
- gain_second: float32 [256], replicated, may hold values from 0.1 to 1.9
- offset_second: float32 [256], replicated, may hold values from -4 to 4
Outputs:
- grad_input: bfloat16 [32, 64, 128, 256], P('tm', 'row', 'col')
All inputs are finite; a program needn't handle non-finite values.
Results may differ from a plain program's by a relative error of at most 0.0035.
The roundings to bfloat16 on the way count: a program that leaves them out, or rounds other values in their place, can miss the bound.
Values may be sent and summed in bfloat16 or wider, within the bound.
A program may use at most 64 MiB of HBM per device.

v0:
```python
import jax
import jax.numpy as jnp
from jax import lax
from jax.sharding import PartitionSpec as P

G = 32


eps_norm = 1e-06


def shifted(value, axis, steps):
    count = lax.axis_size(axis)
    first, last = (max(0, -steps), min(count, count - steps))
    return lax.ppermute(value, axis, [(source, source + steps) for source in range(first, last)])


def with_halo(shard, sides, width):
    for axis, dim in sides:
        count, length = (lax.axis_size(axis), shard.shape[dim])
        up = [(i, (i + 1) % count) for i in range(count - 1)]
        down = [(j, i) for i, j in up]
        last = lax.slice_in_dim(shard, length - width, length, axis=dim)
        first = lax.slice_in_dim(shard, 0, width, axis=dim)
        before = lax.ppermute(last, axis, up)
        after = lax.ppermute(first, axis, down)
        shard = jnp.concatenate([before, shard, after], axis=dim)
    return shard


def prefix_2(part, axis, combine, identity, reverse):
    count = lax.axis_size(axis)
    place = lax.axis_index(axis)
    ahead = count - 1 - place if reverse else place
    gathered = lax.all_gather(part, axis)
    state = jnp.zeros_like(part) + jnp.asarray(identity, part.dtype)

    def one(hop, state):
        source = count - 1 - hop if reverse else hop
        return combine(state, lax.dynamic_index_in_dim(gathered, source, 0, False))

    return lax.fori_loop(0, ahead, one, state)


def convolve(padded, kernel):
    return lax.conv_general_dilated(
        padded[None],
        kernel,
        (1, 1, 1),
        "VALID",
        dimension_numbers=("NDHWC", "DHWIO", "NDHWC"),
        preferred_element_type=jnp.float32,
    )[0]


def flipped(kernel):
    return jnp.swapaxes(kernel[::-1, ::-1, ::-1], 3, 4)


def add_terms(earlier, later):
    return earlier + later


def moments(prefix, counts):
    group_means = prefix[0] / counts
    squares = prefix[1] / counts
    return (group_means, lax.rsqrt(squares - group_means * group_means + eps_norm))


def grad_terms(totals, group_means, inverse_std, counts):
    first_term = (
        -inverse_std * totals[0] + totals[1] * inverse_std * inverse_std * group_means
    ) / counts
    second_term = -0.5 * totals[1] * inverse_std * inverse_std / counts
    return jnp.stack([first_term, second_term])


def reverse_cumsum(terms):
    return jnp.flip(jnp.cumsum(jnp.flip(terms, 1), axis=1), 1)


def build_past(active):
    earlier = shifted(active[-2:], "tm", 1)
    joined = jnp.concatenate([earlier, active], axis=0)
    return with_halo(joined, (("row", 1), ("col", 2)), 1)


def build_future(gradient):
    later = shifted(gradient[:2], "tm", -1)
    joined = jnp.concatenate([gradient, later], axis=0)
    return with_halo(joined, (("row", 1), ("col", 2)), 1)


def frame_setup(values):
    frames_dev = values.shape[0]
    plane_cells = float(
        values.shape[1]
        * values.shape[2]
        * values.shape[4]
        * lax.axis_size("row")
        * lax.axis_size("col")
    )
    first_frame = lax.axis_index("tm") * frames_dev
    own_counts = ((first_frame + jnp.arange(frames_dev) + 1).astype(jnp.float32) * plane_cells)[
        :, None
    ]
    total_frames = frames_dev * lax.axis_size("tm")
    all_counts = ((jnp.arange(total_frames) + 1).astype(jnp.float32) * plane_cells)[:, None]
    return (frames_dev, first_frame, own_counts, all_counts)


def forward_stats(values):
    frames_dev, first_frame, own_counts, all_counts = frame_setup(values)
    local_sums = jnp.stack(
        [jnp.sum(values, axis=(1, 2, 4)), jnp.sum(values * values, axis=(1, 2, 4))]
    )
    totals = lax.psum(local_sums, ("row", "col"))
    carried = prefix_2(
        jnp.sum(totals, axis=1), "tm", add_terms, jnp.zeros((2, G), jnp.float32), False
    )
    prefix = carried[:, None, :] + jnp.cumsum(totals, axis=1)
    own_means, own_inverse = moments(prefix, own_counts)
    return (own_means, own_inverse, own_means, own_inverse)


def backward_stats(grad_hat, normed, stats):
    own_means, own_inverse, all_means, all_inverse = stats
    frames_dev, first_frame, own_counts, all_counts = frame_setup(grad_hat)
    local_sums = jnp.stack(
        [jnp.sum(grad_hat, axis=(1, 2, 4)), jnp.sum(grad_hat * normed, axis=(1, 2, 4))]
    )
    totals = lax.psum(local_sums, ("row", "col"))
    terms = grad_terms(totals, own_means, own_inverse, own_counts)
    carried = prefix_2(
        jnp.sum(terms, axis=1), "tm", add_terms, jnp.zeros((2, G), jnp.float32), True
    )
    return carried[:, None, :] + reverse_cumsum(terms)


def norm_forward(volume, scale_gain, offset):
    values = volume.astype(jnp.float32).reshape(volume.shape[:3] + (G, volume.shape[3] // G))
    stats = forward_stats(values)
    normed = (values - stats[0][:, None, None, :, None]) * stats[1][:, None, None, :, None]
    pre_act = normed * scale_gain.reshape(G, -1) + offset.reshape(G, -1)
    return (values, stats, normed, pre_act)


def norm_backward(grad_act, pre_act, normed, values, scale_gain, stats):
    sigma = jax.nn.sigmoid(pre_act)
    grad_pre = grad_act.reshape(pre_act.shape) * sigma * (1.0 + pre_act * (1.0 - sigma))
    grad_hat = grad_pre * scale_gain.reshape(G, -1)
    suffix = backward_stats(grad_hat, normed, stats)
    result = (
        stats[1][:, None, None, :, None] * grad_hat
        + suffix[0][:, None, None, :, None]
        + 2.0 * values * suffix[1][:, None, None, :, None]
    )
    return result.reshape(grad_act.shape)


def body(
    activations,
    cotangent,
    conv_first,
    bias_first,
    gain_first,
    offset_first,
    conv_second,
    gain_second,
    offset_second,
):
    values_first, stats_first, normed_first, pre_first = norm_forward(
        activations, gain_first, offset_first
    )
    active = jax.nn.silu(pre_first).reshape(activations.shape).astype(jnp.bfloat16)
    hidden = convolve(build_past(active), conv_first)
    layer_out = (activations.astype(jnp.float32) + hidden + bias_first).astype(jnp.bfloat16)
    values_second, stats_second, normed_second, pre_second = norm_forward(
        layer_out, gain_second, offset_second
    )
    grad_second = convolve(build_future(cotangent), flipped(conv_second))
    grad_mid = (
        cotangent.astype(jnp.float32)
        + norm_backward(
            grad_second, pre_second, normed_second, values_second, gain_second, stats_second
        )
    ).astype(jnp.bfloat16)
    grad_first = convolve(build_future(grad_mid), flipped(conv_first))
    return (
        grad_mid.astype(jnp.float32)
        + norm_backward(grad_first, pre_first, normed_first, values_first, gain_first, stats_first)
    ).astype(jnp.bfloat16)


def solution(mesh):
    placed = (
        P("tm", "row", "col", None),
        P("tm", "row", "col", None),
        P(),
        P(),
        P(),
        P(),
        P(),
        P(),
        P(),
    )
    return jax.shard_map(
        body, mesh=mesh, in_specs=placed, out_specs=P("tm", "row", "col", None), check_vma=False
    )
```

profile of v0, /device:TPU:1, one launch (start us, length us, event | category | flops | bytes accessed | tf_op | source)
XLA Modules:
  0.0 498.4 jit_solution(10120412429807136523)
XLA Ops:
  0.0 1.4 convert_reduce_fusion
  4.7 65.3 %psum.28 = f32[2,4,32]{2,1,0:T(4,128)S(1)} all-reduce(f32[2,4,32]{2,1,0:T(4,128)S(1)} %pad_maximum_fusion.15), channel_id=1, replica_groups=mesh['tm'=8,'row'=4,'col'=8] {'row','col'}, use_global_device_ids=true, to_apply=%region_4.5 | all-reduce | flops 256 | bytes 2048 | tf_op jit(solution)/shard_map/psum | solution.py:117
  70.6 13.9 %all-gather.4 = f32[8,2,32]{2,1,0:T(2,128)S(1)} all-gather(f32[1,2,32]{2,1,0:T(2,128)S(1)} %bitcast.161), channel_id=2, replica_groups=mesh['tm'=8,'row'=4,'col'=8] {'tm'}, dimensions={0}, use_global_device_ids=true | all-gather | bytes 2304 | tf_op jit(solution)/shard_map/all_gather | solution.py:35
  89.2 1.5 fusion.63
  92.2 2.1 collective-permute-start
  94.3 1.7 slice.92
  96.0 1.3 collective-permute-start.5
  98.4 1.3 pad_maximum_fusion.6
  99.7 1.3 collective-permute-start.2
  101.0 4.0 collective-permute-start.1
  106.0 1.3 collective-permute-start.7
  107.3 4.0 collective-permute-start.6
  112.1 12.1 %collective-permute-start.4 = (bf16[6,18,1,256]{3,1,2,0:T(8,128)(2,1)S(1)}, bf16[6,18,1,256]{3,1,2,0:T(8,128)(2,1)S(1)}, u32[]{:S(2)}, u32[]{:S(2)}) collective-permute-start(bf16[6,18,1,256]{3,1,2,0:T(8,128)(2,1)S(1)} %get-tuple-element.219), channel_id=1, source_target_pairs={{1,0},{2,1},{3,2},{4,3},{5,4},{6,5},{7,6},{9,8},{10,9},{11,10},{12... | collective-permute-start | bytes 165896 | tf_op jit(solution)/shard_map/ppermute | solution.py:26
  124.2 1.9 collective-permute-start.3
  126.4 2.4 collective-permute-start.9
  128.8 3.2 collective-permute-start.8
  132.0 1.8 maximum_bitcast_fusion
  134.6 6.2 %fusion.30 = f32[4,16,8,3,256]{4,2,3,1,0:T(8,128)S(1)} fusion(bf16[3,3,3,256,256]{4,3,2,1,0:T(8,128)(2,1)S(1)} %copy-done, bf16[6,18,1,7,2,256]{5,3,4,1,0,2:T(8,128)(2,1)S(1)} %slice.119, bf16[6,18,1,8,3,256]{5,3,4,1,0,2:T(8,128)(2,1)S(1)} %copy.28, pred[8,3]{0,1:T(4,128)(4,1)S(1)} %copy-done.19), kind=kOutput, calls=%fused_computation.37 | convolution fusion | flops 5442846720 | bytes 7213080 | tf_op jit(solution)/shard_map/conv_general_dilated | solution.py:46
  140.8 1.6 copy.29
  144.6 4.6 reshape.336
  149.2 2.0 copy.31
  151.7 5.9 %fusion.27 = f32[4,16,8,3,256]{4,2,3,1,0:T(8,128)S(1)} fusion(bf16[3,3,3,256,256]{4,3,2,1,0:T(8,128)(2,1)S(1)} %copy-done.18, bf16[6,18,1,7,2,256]{5,3,4,1,0,2:T(8,128)(2,1)S(1)} %slice.125, bf16[6,18,1,8,3,256]{5,3,4,1,0,2:T(8,128)(2,1)S(1)} %copy.31, pred[8,3]{0,1:T(4,128)(4,1)S(1)} %copy-done.19), kind=kOutput, calls=%fused_computation.36 | convolution fusion | flops 5442846720 | bytes 7213080 | tf_op jit(solution)/shard_map/conv_general_dilated | solution.py:46
  157.7 1.6 copy.32
  159.5 1.7 convert_reduce_fusion.1
  161.2 1.4 reduce_sum.147
  164.2 1.5 reduce_sum.142
  165.7 1.3 pad_maximum_fusion.16
  167.0 61.3 %psum.29 = f32[2,4,32]{2,1,0:T(4,128)S(1)} all-reduce(f32[2,4,32]{2,1,0:T(4,128)} %pad_maximum_fusion.16), channel_id=1, replica_groups=mesh['tm'=8,'row'=4,'col'=8] {'row','col'}, use_global_device_ids=true, to_apply=%region_13.14 | all-reduce | flops 256 | bytes 2048 | tf_op jit(solution)/shard_map/psum | solution.py:117
  229.5 13.7 %all-gather.5 = f32[8,2,32]{2,1,0:T(2,128)} all-gather(f32[1,2,32]{2,1,0:T(2,128)} %bitcast.162), channel_id=3, replica_groups=mesh['tm'=8,'row'=4,'col'=8] {'tm'}, dimensions={0}, use_global_device_ids=true | all-gather | bytes 2304 | tf_op jit(solution)/shard_map/all_gather | solution.py:35
  246.1 1.4 sub.91
  248.4 2.7 fusion.104
  251.1 1.4 reduce_sum.182
  252.5 1.4 reduce_sum.179
  253.9 1.5 reduce_sum.183
  255.4 1.5 reduce_sum.180
  256.9 1.3 pad_maximum_fusion.17
  258.2 68.1 %psum.30 = f32[2,4,32]{2,1,0:T(4,128)} all-reduce(f32[2,4,32]{2,1,0:T(4,128)} %pad_maximum_fusion.17), channel_id=1, replica_groups=mesh['tm'=8,'row'=4,'col'=8] {'row','col'}, use_global_device_ids=true, to_apply=%region_22.23 | all-reduce | flops 256 | bytes 2048 | tf_op jit(solution)/shard_map/psum | solution.py:132
  328.9 1.3 rev.15
  330.2 1.3 reduce_window_sum.27
  331.5 1.3 rev.16
  332.8 17.1 %all-gather.6 = f32[8,2,32]{2,1,0:T(2,128)} all-gather(f32[1,2,32]{2,1,0:T(2,128)} %bitcast.159), channel_id=4, replica_groups=mesh['tm'=8,'row'=4,'col'=8] {'tm'}, dimensions={0}, use_global_device_ids=true | all-gather | bytes 2304 | tf_op jit(solution)/shard_map/all_gather | solution.py:35
  350.4 8.7 %while.46 = (s32[]{:T(128)}, f32[2,32]{1,0:T(2,128)}, s32[]{:T(128)}, f32[8,2,32]{2,1,0:T(2,128)}, s32[]{:T(128)}, /*index=5*/s32[]{:T(128)}, s32[]{:T(128)}, s32[]{:T(128)}) while((s32[]{:T(128)}, f32[2,32]{1,0:T(2,128)}, s32[]{:T(128)}, f32[8,2,32]{2,1,0:T(2,128)}, s32[]{:T(128)}, /*index=5*/s32[]{:T(128)}, s32[]{:T(128)}, ...), condition=%wide.region_25.26_spmd, body=%wide.region_24.25_spmd.sunk | while | flops 70 | bytes 911 | solution.py:42
  361.1 1.5 mul.343
  362.6 1.4 add.292
  364.0 1.5 add.293
  365.5 2.3 fusion.51
  367.9 1.3 collective-permute-start.10
  369.2 5.8 %collective-permute-done.10 = bf16[2,16,16,256]{3,1,2,0:T(8,128)(2,1)S(1)} collective-permute-done((bf16[2,16,16,256]{3,1,2,0:T(8,128)(2,1)S(1)}, bf16[2,16,16,256]{3,1,2,0:T(8,128)(2,1)S(1)}, u32[]{:S(2)}, u32[]{:S(2)}) %collective-permute-start.10) | collective-permute-done | bytes 262176 | tf_op jit(solution)/shard_map/ppermute | solution.py:15
  375.2 1.3 collective-permute-start.12
  376.5 4.0 collective-permute-start.11
  380.5 1.6 collective-permute-done.11
  382.8 8.4 %collective-permute-start.14 = (bf16[6,18,1,256]{3,1,2,0:T(8,128)(2,1)}, bf16[6,18,1,256]{3,1,2,0:T(8,128)(2,1)}, u32[]{:S(2)}, u32[]{:S(2)}) collective-permute-start(bf16[6,18,1,256]{3,1,2,0:T(8,128)(2,1)} %get-tuple-element.217), channel_id=1, source_target_pairs={{1,0},{2,1},{3,2},{4,3},{5,4},{6,5},{7,6},{9,8},{10,9},{11,10},{12... | collective-permute-start | bytes 165896 | tf_op jit(solution)/shard_map/ppermute | solution.py:26
  391.3 2.1 collective-permute-start.13
  393.4 1.5 collective-permute-done.13
  394.9 2.0 maximum_bitcast_fusion.2
  397.8 5.9 %fusion.24 = f32[4,16,8,3,256]{4,2,3,1,0:T(8,128)S(1)} fusion(bf16[3,3,3,256,256]{4,3,2,1,0:T(8,128)(2,1)S(1)} %copy-done, bf16[6,18,1,7,2,256]{5,3,4,1,0,2:T(8,128)(2,1)S(1)} %slice.132, bf16[6,18,1,8,3,256]{5,3,4,1,0,2:T(8,128)(2,1)S(1)} %copy.35, pred[8,3]{0,1:T(4,128)(4,1)S(1)} %copy-done.20), kind=kOutput, calls=%fused_computation.35 | convolution fusion | flops 5442846720 | bytes 7213080 | tf_op jit(solution)/shard_map/conv_general_dilated | solution.py:46
  404.7 1.3 fusion.103
  406.0 1.4 reduce_sum.189
  409.0 1.5 reduce_sum.187
  410.5 1.3 pad_maximum_fusion.19
  411.8 62.0 %psum.31 = f32[2,4,32]{2,1,0:T(4,128)S(1)} all-reduce(f32[2,4,32]{2,1,0:T(4,128)} %pad_maximum_fusion.19), channel_id=1, replica_groups=mesh['tm'=8,'row'=4,'col'=8] {'row','col'}, use_global_device_ids=true, to_apply=%region_31.32 | all-reduce | flops 256 | bytes 2048 | tf_op jit(solution)/shard_map/psum | solution.py:132
  475.9 11.2 %all-gather.7 = f32[8,2,32]{2,1,0:T(2,128)} all-gather(f32[1,2,32]{2,1,0:T(2,128)} %bitcast.160), channel_id=5, replica_groups=mesh['tm'=8,'row'=4,'col'=8] {'tm'}, dimensions={0}, use_global_device_ids=true | all-gather | bytes 2304 | tf_op jit(solution)/shard_map/all_gather | solution.py:35
  487.1 4.7 while.47
  495.1 2.4 fusion.71
  (137 shorter events, 52.9 us)
Async XLA Ops:
  0.0 134.5 %copy-start = (bf16[3,3,3,256,256]{4,3,2,1,0:T(8,128)(2,1)S(1)}, bf16[3,3,3,256,256]{4,3,2,1,0:T(8,128)(2,1)}, u32[]{:S(2)}) copy-start(bf16[3,3,3,256,256]{4,3,2,1,0:T(8,128)(2,1)} %param.19) | copy-start | bytes 10616836
  84.6 159.3 %copy-start.14 = (f32[4]{0:T(128)}, f32[4]{0:T(128)S(1)}, u32[]{:S(2)}) copy-start(f32[4]{0:T(128)S(1)} %convert_multiply_fusion.4) | copy-start | bytes 52
  85.3 0.6 copy-start.11
  90.7 0.8 copy-start.4
  92.2 6.2 %collective-permute-start = (bf16[2,16,16,256]{3,1,2,0:T(8,128)(2,1)}, bf16[2,16,16,256]{3,1,2,0:T(8,128)(2,1)}, u32[]{:S(2)}, u32[]{:S(2)}) collective-permute-start(bf16[2,16,16,256]{3,1,2,0:T(8,128)(2,1)} %slice.118), channel_id=1, source_target_pairs={{0,32},{32,64},{64,96},{96,128},{128,160},{160,192},{192,224},{1,3... | collective-permute-start | bytes 786440 | tf_op jit(solution)/shard_map/ppermute | solution.py:15
  96.0 9.0 %collective-permute-start.5 = (bf16[2,16,16,256]{3,2,1,0:T(8,128)(2,1)}, bf16[2,16,16,256]{3,2,1,0:T(8,128)(2,1)}, u32[]{:S(2)}, u32[]{:S(2)}) collective-permute-start(bf16[2,16,16,256]{3,2,1,0:T(8,128)(2,1)} %slice.92), channel_id=1, source_target_pairs={{32,0},{64,32},{96,64},{128,96},{160,128},{192,160},{224,192},{33,... | collective-permute-start | bytes 786440 | tf_op jit(solution)/shard_map/ppermute | solution.py:15
  97.3 14.1 %copy-start.5 = (bf16[4,16,16,256]{3,1,2,0:T(8,128)(2,1)S(1)}, bf16[4,16,16,256]{3,1,2,0:T(8,128)(2,1)}, u32[]{:S(2)}) copy-start(bf16[4,16,16,256]{3,1,2,0:T(8,128)(2,1)} %copy-done.4) | copy-start | bytes 1572868
  99.7 11.6 %collective-permute-start.2 = (bf16[6,1,16,256]{3,1,2,0:T(2,128)(2,1)S(1)}, bf16[6,1,16,256]{3,1,2,0:T(2,128)(2,1)S(1)}, u32[]{:S(2)}, u32[]{:S(2)}) collective-permute-start(bf16[6,1,16,256]{3,1,2,0:T(2,128)(2,1)S(1)} %get-tuple-element.227), channel_id=1, source_target_pairs={{8,0},{16,8},{24,16},{9,1},{17,9},{25,17},{10,2},{18,10},{26,18},{... | collective-permute-start | bytes 147464 | tf_op jit(solution)/shard_map/ppermute | solution.py:26
  101.0 10.3 %collective-permute-start.1 = (bf16[6,1,16,256]{3,1,2,0:T(2,128)(2,1)S(1)}, bf16[6,1,16,256]{3,1,2,0:T(2,128)(2,1)S(1)}, u32[]{:S(2)}, u32[]{:S(2)}) collective-permute-start(bf16[6,1,16,256]{3,1,2,0:T(2,128)(2,1)S(1)} %get-tuple-element.226), channel_id=1, source_target_pairs={{0,8},{8,16},{16,24},{1,9},{9,17},{17,25},{2,10},{10,18},{18,26},{... | collective-permute-start | bytes 147464 | tf_op jit(solution)/shard_map/ppermute | solution.py:25
  106.0 20.2 %collective-permute-start.7 = (bf16[6,1,16,256]{3,2,1,0:T(8,128)(2,1)S(1)}, bf16[6,1,16,256]{3,2,1,0:T(8,128)(2,1)S(1)}, u32[]{:S(2)}, u32[]{:S(2)}) collective-permute-start(bf16[6,1,16,256]{3,2,1,0:T(8,128)(2,1)S(1)} %get-tuple-element.225), channel_id=1, source_target_pairs={{8,0},{16,8},{24,16},{9,1},{17,9},{25,17},{10,2},{18,10},{26,18},{... | collective-permute-start | bytes 147464 | tf_op jit(solution)/shard_map/ppermute | solution.py:26
  107.3 18.9 %collective-permute-start.6 = (bf16[6,1,16,256]{3,2,1,0:T(8,128)(2,1)S(1)}, bf16[6,1,16,256]{3,2,1,0:T(8,128)(2,1)S(1)}, u32[]{:S(2)}, u32[]{:S(2)}) collective-permute-start(bf16[6,1,16,256]{3,2,1,0:T(8,128)(2,1)S(1)} %get-tuple-element.224), channel_id=1, source_target_pairs={{0,8},{8,16},{16,24},{1,9},{9,17},{17,25},{2,10},{10,18},{18,26},{... | collective-permute-start | bytes 147464 | tf_op jit(solution)/shard_map/ppermute | solution.py:25
  112.1 19.8 %collective-permute-start.4 = (bf16[6,18,1,256]{3,1,2,0:T(8,128)(2,1)S(1)}, bf16[6,18,1,256]{3,1,2,0:T(8,128)(2,1)S(1)}, u32[]{:S(2)}, u32[]{:S(2)}) collective-permute-start(bf16[6,18,1,256]{3,1,2,0:T(8,128)(2,1)S(1)} %get-tuple-element.219), channel_id=1, source_target_pairs={{1,0},{2,1},{3,2},{4,3},{5,4},{6,5},{7,6},{9,8},{10,9},{11,10},{12... | collective-permute-start | bytes 165896 | tf_op jit(solution)/shard_map/ppermute | solution.py:26
  124.2 7.7 %collective-permute-start.3 = (bf16[6,18,1,256]{3,1,2,0:T(8,128)(2,1)S(1)}, bf16[6,18,1,256]{3,1,2,0:T(8,128)(2,1)S(1)}, u32[]{:S(2)}, u32[]{:S(2)}) collective-permute-start(bf16[6,18,1,256]{3,1,2,0:T(8,128)(2,1)S(1)} %get-tuple-element.218), channel_id=1, source_target_pairs={{0,1},{1,2},{2,3},{3,4},{4,5},{5,6},{6,7},{8,9},{9,10},{10,11},{11... | collective-permute-start | bytes 165896 | tf_op jit(solution)/shard_map/ppermute | solution.py:25
  126.4 16.1 %collective-permute-start.9 = (bf16[6,18,1,256]{3,2,1,0:T(2,128)(2,1)S(1)}, bf16[6,18,1,256]{3,2,1,0:T(2,128)(2,1)S(1)}, u32[]{:S(2)}, u32[]{:S(2)}) collective-permute-start(bf16[6,18,1,256]{3,2,1,0:T(2,128)(2,1)S(1)} %get-tuple-element.221), channel_id=1, source_target_pairs={{1,0},{2,1},{3,2},{4,3},{5,4},{6,5},{7,6},{9,8},{10,9},{11,10},{12... | collective-permute-start | bytes 165896 | tf_op jit(solution)/shard_map/ppermute | solution.py:26
  128.8 13.7 %collective-permute-start.8 = (bf16[6,18,1,256]{3,2,1,0:T(2,128)(2,1)S(1)}, bf16[6,18,1,256]{3,2,1,0:T(2,128)(2,1)S(1)}, u32[]{:S(2)}, u32[]{:S(2)}) collective-permute-start(bf16[6,18,1,256]{3,2,1,0:T(2,128)(2,1)S(1)} %get-tuple-element.220), channel_id=1, source_target_pairs={{0,1},{1,2},{2,3},{3,4},{4,5},{5,6},{6,7},{8,9},{9,10},{10,11},{11... | collective-permute-start | bytes 165896 | tf_op jit(solution)/shard_map/ppermute | solution.py:25
  133.9 0.7 copy-start.19
  149.2 2.5 copy-start.18
  157.6 1.7 copy-start.2
  157.6 1.9 copy-start.7
  157.6 1.9 copy-start.17
  243.8 0.7 copy-start.13
  367.8 14.3 %copy-start.1 = (bf16[4,16,16,256]{3,1,2,0:T(8,128)(2,1)}, bf16[4,16,16,256]{3,1,2,0:T(8,128)(2,1)S(1)}, u32[]{:S(2)}) copy-start(bf16[4,16,16,256]{3,1,2,0:T(8,128)(2,1)S(1)} %fusion.51) | copy-start | bytes 1572868
  367.9 7.1 %collective-permute-start.10 = (bf16[2,16,16,256]{3,1,2,0:T(8,128)(2,1)S(1)}, bf16[2,16,16,256]{3,1,2,0:T(8,128)(2,1)S(1)}, u32[]{:S(2)}, u32[]{:S(2)}) collective-permute-start(bf16[2,16,16,256]{3,1,2,0:T(8,128)(2,1)S(1)} %slice.131), channel_id=1, source_target_pairs={{32,0},{64,32},{96,64},{128,96},{160,128},{192,160},{224,192},{33,... | collective-permute-start | bytes 786440 | tf_op jit(solution)/shard_map/ppermute | solution.py:15
  375.0 7.8 %copy-start.8 = (bf16[2,16,16,256]{3,1,2,0:T(8,128)(2,1)}, bf16[2,16,16,256]{3,1,2,0:T(8,128)(2,1)S(1)}, u32[]{:S(2)}) copy-start(bf16[2,16,16,256]{3,1,2,0:T(8,128)(2,1)S(1)} %collective-permute-done.10) | copy-start | bytes 786436
  375.2 5.4 %collective-permute-start.12 = (bf16[6,1,16,256]{3,1,2,0:T(2,128)(2,1)S(1)}, bf16[6,1,16,256]{3,1,2,0:T(2,128)(2,1)S(1)}, u32[]{:S(2)}, u32[]{:S(2)}) collective-permute-start(bf16[6,1,16,256]{3,1,2,0:T(2,128)(2,1)S(1)} %get-tuple-element.223), channel_id=1, source_target_pairs={{8,0},{16,8},{24,16},{9,1},{17,9},{25,17},{10,2},{18,10},{26,18},{... | collective-permute-start | bytes 147464 | tf_op jit(solution)/shard_map/ppermute | solution.py:26
  376.5 5.6 %collective-permute-start.11 = (bf16[6,1,16,256]{3,1,2,0:T(2,128)(2,1)S(1)}, bf16[6,1,16,256]{3,1,2,0:T(2,128)(2,1)S(1)}, u32[]{:S(2)}, u32[]{:S(2)}) collective-permute-start(bf16[6,1,16,256]{3,1,2,0:T(2,128)(2,1)S(1)} %get-tuple-element.222), channel_id=1, source_target_pairs={{0,8},{8,16},{16,24},{1,9},{9,17},{17,25},{2,10},{10,18},{18,26},{... | collective-permute-start | bytes 147464 | tf_op jit(solution)/shard_map/ppermute | solution.py:25
  380.5 2.3 copy-start.9
  382.1 9.2 %copy-start.10 = (bf16[6,1,16,256]{3,1,2,0:T(2,128)(2,1)}, bf16[6,1,16,256]{3,1,2,0:T(2,128)(2,1)S(1)}, u32[]{:S(2)}) copy-start(bf16[6,1,16,256]{3,1,2,0:T(2,128)(2,1)S(1)} %collective-permute-done.11) | copy-start | bytes 147460
  382.8 10.6 %collective-permute-start.14 = (bf16[6,18,1,256]{3,1,2,0:T(8,128)(2,1)}, bf16[6,18,1,256]{3,1,2,0:T(8,128)(2,1)}, u32[]{:S(2)}, u32[]{:S(2)}) collective-permute-start(bf16[6,18,1,256]{3,1,2,0:T(8,128)(2,1)} %get-tuple-element.217), channel_id=1, source_target_pairs={{1,0},{2,1},{3,2},{4,3},{5,4},{6,5},{7,6},{9,8},{10,9},{11,10},{12... | collective-permute-start | bytes 165896 | tf_op jit(solution)/shard_map/ppermute | solution.py:26
  391.3 3.6 collective-permute-start.13
  397.1 0.7 copy-start.20
  403.6 1.0 copy-start.3
  403.6 1.0 copy-start.15
  403.6 1.0 copy-start.16
  403.7 70.2 %copy-start.12 = (f32[2,4,32]{2,1,0:T(4,128)S(1)}, f32[2,4,32]{2,1,0:T(4,128)}, u32[]{:S(2)}) copy-start(f32[2,4,32]{2,1,0:T(4,128)} %copy-done.11) | copy-start | bytes 3076
  404.2 1.8 copy-start.6
where the time goes:
time: 503 us; the launch traced here: 498 us
  blocking collectives  312 us (62%)
  other arithmetic  59.3 us (12%)
  starting transfers between devices  50.7 us (10%)
  local copies, waits for them, and re-layouts  48.4 us (10%)
  matrix products  18 us (4%)
  waiting for transfers between devices  8.93 us (2%)
    psum x2, blocking collectives, backward_stats(): totals = lax.psum(local_sums, ('row', 'col'))  130 us
    psum x2, blocking collectives, forward_stats(): totals = lax.psum(local_sums, ('row', 'col'))  127 us
    all_gather x4, blocking collectives, prefix_2(): gathered = lax.all_gather(part, axis)  55.8 us
    ppermute x6, starting transfers between devices, with_halo(): after = lax.ppermute(first, axis, down)  26.8 us
    ppermute x6, starting transfers between devices, with_halo(): before = lax.ppermute(last, axis, up)  19.2 us
    conv_general_dilated x3, matrix products, convolve(): lax.conv_general_dilated(padded[None], kernel, (1, 1, 1), 'VALID', dimens...  18 us
    add x14, other arithmetic, add_terms(): return earlier + later  13.4 us
    conv_general_dilated x10, local copies, waits for them, and re-layouts, convolve(): lax.conv_general_dilated(padded[None], kernel, (1, 1, 1), 'VALID', dimens...  11.5 us
  transfers between devices with their start and end apart: 15, of which 4 were waited for; matrix products, arithmetic and copies ran while one was open for 3% of the time, Pallas kernels for 0%

commit v1 on v0

v1 whole, which is shorter than its diff:
```python
import functools
import itertools

import jax
import jax.numpy as jnp
from jax import lax
from jax.experimental import pallas as pl
from jax.experimental.pallas import tpu as pltpu
from jax.sharding import PartitionSpec as P

MESH = pl.DeviceIdType.MESH
BF16, F32 = jnp.bfloat16, jnp.float32
EPS = 1e-6
F, H, W, C, G = 4, 16, 16, 256, 32
TAPS = tuple(itertools.product(range(3), repeat=3))
AXES = ("tm", "row", "col")


def offsets_of(sizes):
    tms, rows, cols = sizes
    plane = [(0, b, d) for b in range(rows) for d in range(cols) if (b, d) != (0, 0)]
    plane.sort(key=lambda o: -(min(o[1], rows - o[1]) + min(o[2], cols - o[2])))
    line = [(a, 0, 0) for a in range(1, tms)]
    rims = [
        (a % tms, b % rows, d % cols)
        for a in (-1, 1)
        for b in (-1, 0, 1)
        for d in (-1, 0, 1)
    ]
    everyone = list(dict.fromkeys(plane + line + rims))
    return plane, line, everyone


def sigmoid(u):
    return 0.5 * jnp.tanh(0.5 * u) + 0.5


def split3(x):
    high = x.astype(BF16)
    rest = x - high.astype(F32)
    middle = rest.astype(BF16)
    low = (rest - middle.astype(F32)).astype(BF16)
    return jnp.concatenate([high, middle, low], axis=0)


def exact_dot(x, picks):
    n = x.shape[0]
    y = jnp.dot(split3(x), picks, preferred_element_type=F32)
    return y[:n] + y[n : 2 * n] + y[2 * n :]


def frame_of_lane(shape):
    return lax.broadcasted_iota(jnp.int32, shape, len(shape) - 1) >> 5


def over_frames(x):
    return x + pltpu.roll(x, 32, 1) + pltpu.roll(x, 64, 1) + pltpu.roll(x, 96, 1)


def running(x):
    f = frame_of_lane(x.shape)
    return (
        x
        + jnp.where(f >= 1, pltpu.roll(x, 32, 1), 0.0)
        + jnp.where(f >= 2, pltpu.roll(x, 64, 1), 0.0)
        + jnp.where(f >= 3, pltpu.roll(x, 96, 1), 0.0)
    )


def running_back(x):
    f = frame_of_lane(x.shape)
    return (
        x
        + jnp.where(f <= 2, pltpu.roll(x, 96, 1), 0.0)
        + jnp.where(f <= 1, pltpu.roll(x, 64, 1), 0.0)
        + jnp.where(f <= 0, pltpu.roll(x, 32, 1), 0.0)
    )


def kernel(
    sizes,
    act_hbm,
    cot_hbm,
    w1_hbm,
    w2_hbm,
    bias1,
    gain1,
    offset1,
    gain2,
    offset2,
    out_ref,
    actf,
    cotf,
    gmf,
    w1,
    w2,
    taps,
    grad,
    lay,
    stage,
    colpack,
    cornerpack,
    colhalo,
    cornerhalo,
    colside,
    part,
    gather_m,
    spread_m,
    stat1,
    stat2,
    ends,
    mine,
    line_mine,
    plane_in,
    line_in,
    in_sem,
    halo_send,
    halo_recv,
    plane_send,
    plane_recv,
    line_send,
    line_recv,
):
    tms, rows, cols = sizes
    t, r, c = (lax.axis_index(a) for a in AXES)
    plane, line, everyone = offsets_of(sizes)
    plane_cells = float(H * rows * W * cols * (C // G))

    def at(o):
        return (
            lax.rem(t + (o[0] % tms), tms),
            lax.rem(r + (o[1] % rows), rows),
            lax.rem(c + (o[2] % cols), cols),
        )

    barrier = pltpu.get_barrier_semaphore()
    for o in everyone:
        pl.semaphore_signal(barrier, inc=1, device_id=at(o), device_id_type=MESH)

    loads = [
        pltpu.make_async_copy(act_hbm, actf.at[pl.ds(2, F), pl.ds(1, H)], in_sem.at[0]),
        pltpu.make_async_copy(cot_hbm, cotf.at[pl.ds(0, F), pl.ds(1, H)], in_sem.at[1]),
        pltpu.make_async_copy(w1_hbm, w1, in_sem.at[2]),
        pltpu.make_async_copy(w2_hbm, w2, in_sem.at[3]),
    ]
    for load in loads:
        load.start()

    channel = lax.broadcasted_iota(jnp.int32, (C, 128), 0) >> 3
    group = lax.broadcasted_iota(jnp.int32, (C, 128), 1) & (G - 1)
    gather_m[...] = jnp.where(channel == group, 1.0, 0.0).astype(BF16)
    channel = lax.broadcasted_iota(jnp.int32, (128, C), 1) >> 3
    group = lax.broadcasted_iota(jnp.int32, (128, C), 0) & (G - 1)
    spread_m[...] = jnp.where(channel == group, 1.0, 0.0).astype(BF16)

    def packed_sums():
        y = exact_dot(part[...].reshape(2 * F * 8, C), gather_m[...])
        y = y.reshape(2, F, 8, 128)
        f = frame_of_lane((2, 8, 128))
        z = jnp.zeros((2, 8, 128), F32)
        for i in range(F):
            z = z + jnp.where(f == i, y[:, i], 0.0)
        return jnp.sum(z, axis=1)

    def plane_copy(k, j):
        return pltpu.make_async_remote_copy(
            src_ref=mine.at[k],
            dst_ref=plane_in.at[k, j],
            send_sem=plane_send.at[k],
            recv_sem=plane_recv.at[k],
            device_id=at(plane[j]),
            device_id_type=MESH,
        )

    def line_copy(k, j):
        return pltpu.make_async_remote_copy(
            src_ref=line_mine.at[k],
            dst_ref=line_in.at[k, j],
            send_sem=line_send.at[k],
            recv_sem=line_recv.at[k],
            device_id=at(line[j]),
            device_id_type=MESH,
        )

    def await_all(buffer, sem):
        pltpu.make_async_copy(buffer, buffer, sem).wait()

    def plane_start(k):
        mine[k] = packed_sums()
        for j in range(len(plane)):
            plane_copy(k, j).start()

    def plane_end(k):
        await_all(plane_in.at[k], plane_recv.at[k])
        return mine[k] + jnp.sum(plane_in[k], axis=0)

    def line_start(k, value):
        line_mine[k] = value
        for j in range(len(line)):
            line_copy(k, j).start()

    def line_end(k):
        await_all(line_in.at[k], line_recv.at[k])
        return [line_in[k, j] for j in range(len(line))]

    def counts(first_frame):
        f = first_frame + frame_of_lane((1, 128)) + 1
        return jnp.maximum(f, 1).astype(F32) * plane_cells

    def moments(prefix, n):
        mean = prefix[0:1] / n
        return mean, lax.rsqrt(prefix[1:2] / n - mean * mean + EPS)

    def spread(first, second, before=None):
        row = lax.broadcasted_iota(jnp.int32, (8, 128), 0)
        f = frame_of_lane((8, 128))
        halves = []
        for i, own in enumerate((first, second)):
            own = jnp.broadcast_to(own, (8, 128))
            if before is None:
                halves.append(jnp.where(f == row, own, 0.0))
            else:
                ahead = jnp.broadcast_to(before[i], (8, 128))
                frame = jnp.where(row < 2, row + 2, row - 2)
                halves.append(jnp.where(f == frame, jnp.where(row < 2, ahead, own), 0.0))
        return exact_dot(jnp.concatenate(halves, axis=0), spread_m[...])

    def forward_end(k, layer):
        got = line_end(k)
        zero = jnp.zeros((2, 128), F32)
        near = jnp.where(t >= 1, got[0], zero)
        far = zero
        for j in range(1, len(line)):
            far = far + jnp.where(t >= j + 1, got[j], zero)
        own = moments(over_frames(far + near) + running(line_mine[k]), counts(t * F))
        ends[layer, 0:1] = own[0]
        ends[layer, 1:2] = own[1]
        before = None
        if layer == 0:
            before = moments(over_frames(far) + running(near), counts(t * F - F))
        return spread(own[0], own[1], before)

    def backward_terms(k, layer):
        totals = plane_end(k)
        mean, inverse = ends[layer, 0:1], ends[layer, 1:2]
        n = counts(t * F)
        a, b = totals[0:1], totals[1:2]
        first = (-inverse * a + b * inverse * inverse * mean) / n
        second = -0.5 * b * inverse * inverse / n
        return jnp.concatenate([first, second], axis=0)

    def backward_end(k):
        got = line_end(k)
        zero = jnp.zeros((2, 128), F32)
        later = zero
        for j in range(len(line)):
            later = later + jnp.where(t < j + 1, got[j], zero)
        rest = over_frames(later) + running_back(line_mine[k])
        return spread(rest[0:1], rest[1:2])

    def put_stage(start, x):
        for i in range(2):
            stage[i, pl.ds(start, x.shape[0])] = x[:, i * 128 : i * 128 + 128]

    def staged(start, size, stride):
        return jnp.concatenate(
            [stage[i, pl.ds(start, size, stride=stride), :] for i in range(2)], axis=1
        )

    def pack_rims(k):
        for side, column in enumerate((0, W - 1)):
            for f in range(F):
                rim = staged(f * H * W + column, H, W)
                colpack[k, side, f] = rim.astype(BF16)
            for end, line_at in enumerate((0, H - 1)):
                cornerpack[k, end, side] = staged(line_at * W + column, F, H * W)

    def rim_copies(k, full, own, halo, turn):
        last = own + (F - 2 if turn > 0 else 0)
        inner = F - 2 if turn > 0 else 0
        moves = [((turn, 0, 0), full.at[pl.ds(last, 2), pl.ds(1, H)], full.at[pl.ds(halo, 2), pl.ds(1, H)])]
        for step, src, dst in ((1, H, 0), (-1, 1, H + 1)):
            moves.append(((0, step, 0), full.at[pl.ds(own, F), src], full.at[pl.ds(own, F), dst]))
            moves.append(((turn, step, 0), full.at[pl.ds(last, 2), src], full.at[pl.ds(halo, 2), dst]))
        for step, src, dst in ((1, 1, 0), (-1, 0, 1)):
            moves.append(((0, 0, step), colpack.at[k, src], colhalo.at[k, dst, pl.ds(own, F)]))
            moves.append(
                ((turn, 0, step), colpack.at[k, src, pl.ds(inner, 2)], colhalo.at[k, dst, pl.ds(halo, 2)])
            )
        for down, over in itertools.product((1, -1), repeat=2):
            src = cornerpack.at[k, int(down > 0), int(over > 0)]
            place = (int(down < 0), int(over < 0))
            moves.append(((0, down, over), src, cornerhalo.at[k, 0, place[0], place[1]]))
            moves.append(((turn, down, over), src, cornerhalo.at[k, 1, place[0], place[1]]))
        return [
            pltpu.make_async_remote_copy(
                src_ref=src,
                dst_ref=dst,
                send_sem=halo_send.at[k, j],
                recv_sem=halo_recv.at[k, j],
                device_id=at(o),
                device_id_type=MESH,
            )
            for j, (o, src, dst) in enumerate(moves)
        ]

    def side_columns(k, own, halo, turn, change):
        inner = F - 2 if turn > 0 else 0
        for side in range(2):

            def one(f, carry, side=side):
                colside[side, f, pl.ds(1, H)] = change(colhalo[k, side, f].astype(F32), f)
                return carry

            lax.fori_loop(0, F + 2, one, 0)
            for end, place in ((0, 0), (1, H + 1)):
                for f in range(F):
                    value = cornerhalo[k, 0, end, side, pl.ds(f, 1)]
                    colside[side, own + f, pl.ds(place, 1)] = change(value, own + f)
                for f in range(2):
                    value = cornerhalo[k, 1, end, side, pl.ds(inner + f, 1)]
                    colside[side, halo + f, pl.ds(place, 1)] = change(value, halo + f)

        @pl.when(c == 0)
        def _():
            colside[0] = jnp.zeros(colside.shape[1:], F32)

        @pl.when(c == cols - 1)
        def _():
            colside[1] = jnp.zeros(colside.shape[1:], F32)

    def build(full, halo, edge, change):
        column = lax.broadcasted_iota(jnp.int32, (6, W, C), 1)

        def one(f, carry):
            for h in range(0, H + 2, 6):
                x = change(full[f, pl.ds(h, 6)].astype(F32), f)
                left = colside[0, f, pl.ds(h, 6)].reshape(6, 1, C)
                right = colside[1, f, pl.ds(h, 6)].reshape(6, 1, C)
                taps[1, f, pl.ds(h, 6)] = x.astype(BF16)
                taps[0, f, pl.ds(h, 6)] = jnp.where(
                    column == 0, left, pltpu.roll(x, 1, 1)
                ).astype(BF16)
                taps[2, f, pl.ds(h, 6)] = jnp.where(
                    column == W - 1, right, pltpu.roll(x, W - 1, 1)
                ).astype(BF16)
            return carry

        lax.fori_loop(0, F + 2, one, 0)

        @pl.when(r == 0)
        def _():
            taps[:, :, 0] = jnp.zeros((3, F + 2, W, C), BF16)

        @pl.when(r == rows - 1)
        def _():
            taps[:, :, H + 1] = jnp.zeros((3, F + 2, W, C), BF16)

        @pl.when(t == edge)
        def _():
            for f in range(2):
                for dw in range(3):
                    taps[dw, halo + f] = jnp.zeros((H + 2, W, C), BF16)

    def convolve(f, weights, back):
        left = jnp.concatenate(
            [
                taps[dw, pl.ds(f + dt, 2), pl.ds(dh, H)].reshape(2 * H * W, C)
                for dt, dh, dw in TAPS
            ],
            axis=1,
        )
        if back:
            right = jnp.concatenate([weights[26 - n] for n in range(27)], axis=1)
            return lax.dot_general(left, right, (((1,), (1,)), ((), ())), preferred_element_type=F32)
        return jnp.dot(left, weights[...].reshape(27 * C, C), preferred_element_type=F32)

    def row_of(ref, i):
        return ref[pl.ds(i, 1), :]

    def sums(x):
        return jnp.sum(x.reshape(-1, 8, C), axis=0)

    def norm_grad(values, d, mean, inverse, gain, offset):
        normed = (values - mean) * inverse
        pre = normed * gain + offset
        s = sigmoid(pre)
        e = d * s * (1.0 + pre * (1.0 - s)) * gain
        return e, sums(e), sums(e * normed)

    vectors = [ref[...].reshape(1, C) for ref in (bias1, gain1, offset1, gain2, offset2)]
    bias1, gain1, offset1, gain2, offset2 = vectors

    loads[0].wait()

    def first_sums(f, carry):
        x = actf[f + 2, pl.ds(1, H)].astype(F32).reshape(H * W, C)
        put_stage(f * H * W, x)
        part[0, f] = sums(x)
        part[1, f] = sums(x * x)
        return carry

    lax.fori_loop(0, F, first_sums, 0)
    pack_rims(0)
    pl.semaphore_wait(barrier, len(everyone))
    plane_start(0)
    past = rim_copies(0, actf, 2, 0, 1)
    for copy in past:
        copy.start()
    loads[1].wait()

    def to_stage(f, carry):
        put_stage(f * H * W, cotf[f, pl.ds(1, H)].astype(F32).reshape(H * W, C))
        return carry

    lax.fori_loop(0, F, to_stage, 0)
    pack_rims(1)
    future = rim_copies(1, cotf, 0, 4, -1)
    for copy in future:
        copy.start()
    line_start(0, plane_end(0))
    stat1[...] = forward_end(0, 0)

    for copy in past:
        copy.wait_recv()

    def activate(x, f):
        shape = (1,) * (x.ndim - 1) + (C,)
        mean = row_of(stat1, f).reshape(shape)
        inverse = row_of(stat1, f + 8).reshape(shape)
        u = (x - mean) * inverse * gain1.reshape(shape) + offset1.reshape(shape)
        return u * sigmoid(u)

    side_columns(0, 2, 0, 1, activate)
    build(actf, 0, 0, activate)
    loads[2].wait()

    def first_layer(i, carry):
        f = 2 * i
        hidden = convolve(f, w1, False)
        x = actf[pl.ds(f + 2, 2), pl.ds(1, H)].astype(F32).reshape(2 * H * W, C)
        y = (x + hidden + bias1).astype(BF16)
        lay[pl.ds(f, 2)] = y.reshape(2, H, W, C)
        y = y.astype(F32)
        for j in range(2):
            z = y[j * H * W : (j + 1) * H * W]
            part[0, f + j] = sums(z)
            part[1, f + j] = sums(z * z)
        return carry

    lax.fori_loop(0, F // 2, first_layer, 0)
    plane_start(1)

    for copy in future:
        copy.wait_recv()
    loads[3].wait()
    same = lambda x, f: x
    side_columns(1, 0, 4, -1, same)
    build(cotf, 4, tms - 1, same)

    def second_grad(f):
        grad[pl.ds(f, 2)] = convolve(f, w2, True).reshape(2, H, W, C)

    second_grad(0)
    line_start(1, plane_end(1))
    second_grad(2)
    stat2[...] = forward_end(1, 1)

    def second_norm(f, carry):
        mean, inverse = row_of(stat2, f), row_of(stat2, f + 8)
        a = b = jnp.zeros((8, C), F32)
        for h in range(0, H, 8):
            v = lay[f, pl.ds(h, 8)].astype(F32).reshape(8 * W, C)
            d = grad[f, pl.ds(h, 8)].reshape(8 * W, C)
            e, da, db = norm_grad(v, d, mean, inverse, gain2, offset2)
            grad[f, pl.ds(h, 8)] = e.reshape(8, W, C)
            a, b = a + da, b + db
        part[0, f] = a
        part[1, f] = b
        return carry

    lax.fori_loop(0, F, second_norm, 0)
    plane_start(2)
    line_start(2, backward_terms(2, 1))
    rest2 = backward_end(2)
    ends_rows = stat2[8:16]
    stat2[0:8] = ends_rows
    part[0, 0] = rest2[0:8]
    part[0, 1] = rest2[8:16]

    def middle(f, carry):
        inverse = row_of(stat2, f)
        r1 = part[0, 0, pl.ds(f, 1)]
        r2 = part[0, 1, pl.ds(f, 1)]
        for h in range(0, H, 8):
            v = lay[f, pl.ds(h, 8)].astype(F32).reshape(8 * W, C)
            e = grad[f, pl.ds(h, 8)].reshape(8 * W, C)
            x = cotf[f, pl.ds(h + 1, 8)].astype(F32).reshape(8 * W, C)
            y = (x + (inverse * e + r1 + 2.0 * v * r2)).astype(BF16)
            gmf[f, pl.ds(h + 1, 8)] = y.reshape(8, W, C)
            put_stage(f * H * W + h * W, y.astype(F32))
        return carry

    lax.fori_loop(0, F, middle, 0)
    pack_rims(2)
    middle_rims = rim_copies(2, gmf, 0, 4, -1)
    for copy in middle_rims:
        copy.start()
    for copy in middle_rims:
        copy.wait_recv()

    side_columns(2, 0, 4, -1, same)
    build(gmf, 4, tms - 1, same)

    def first_grad(i, carry):
        f = 2 * i
        grad[pl.ds(f, 2)] = convolve(f, w1, True).reshape(2, H, W, C)
        return carry

    lax.fori_loop(0, F // 2, first_grad, 0)

    def first_norm(f, carry):
        mean, inverse = row_of(stat1, f + 2), row_of(stat1, f + 10)
        a = b = jnp.zeros((8, C), F32)
        for h in range(0, H, 8):
            v = actf[f + 2, pl.ds(h + 1, 8)].astype(F32).reshape(8 * W, C)
            d = grad[f, pl.ds(h, 8)].reshape(8 * W, C)
            e, da, db = norm_grad(v, d, mean, inverse, gain1, offset1)
            grad[f, pl.ds(h, 8)] = e.reshape(8, W, C)
            a, b = a + da, b + db
        part[0, f] = a
        part[1, f] = b
        return carry

    lax.fori_loop(0, F, first_norm, 0)
    plane_start(3)
    line_start(3, backward_terms(3, 0))
    rest1 = backward_end(3)
    part[0, 0] = rest1[0:8]
    part[0, 1] = rest1[8:16]

    def finish(f, carry):
        inverse = row_of(stat1, f + 10)
        r1 = part[0, 0, pl.ds(f, 1)]
        r2 = part[0, 1, pl.ds(f, 1)]
        for h in range(0, H, 8):
            v = actf[f + 2, pl.ds(h + 1, 8)].astype(F32).reshape(8 * W, C)
            e = grad[f, pl.ds(h, 8)].reshape(8 * W, C)
            x = gmf[f, pl.ds(h + 1, 8)].astype(F32).reshape(8 * W, C)
            y = x + (inverse * e + r1 + 2.0 * v * r2)
            out_ref[f, pl.ds(h, 8)] = y.astype(BF16).reshape(8, W, C)
        return carry

    lax.fori_loop(0, F, finish, 0)

    for copy in past + future + middle_rims:
        copy.wait_send()
    for k in range(4):
        await_all(plane_in.at[k], plane_send.at[k])
        await_all(line_in.at[k], line_send.at[k])


def solution(mesh):
    sizes = tuple(mesh.shape[a] for a in AXES)
    n_plane, n_line = sizes[1] * sizes[2] - 1, sizes[0] - 1
    rims = 17
    full = (F + 2, H + 2, W, C)

    def step(act, cot, w1, b1, g1, o1, w2, g2, o2):
        hbm = pl.BlockSpec(memory_space=pl.ANY)
        vmem = pl.BlockSpec(memory_space=pltpu.VMEM)
        return pl.pallas_call(
            functools.partial(kernel, sizes),
            name="vae_grad",
            out_shape=jax.ShapeDtypeStruct((F, H, W, C), BF16),
            in_specs=[hbm] * 4 + [vmem] * 5,
            out_specs=vmem,
            scratch_shapes=[
                pltpu.VMEM(full, BF16),
                pltpu.VMEM(full, BF16),
                pltpu.VMEM(full, BF16),
                pltpu.VMEM((27, C, C), BF16),
                pltpu.VMEM((27, C, C), BF16),
                pltpu.VMEM((3,) + full, BF16),
                pltpu.VMEM((F, H, W, C), F32),
                pltpu.VMEM((F, H, W, C), BF16),
                pltpu.VMEM((2, F * H * W, 128), F32),
                pltpu.VMEM((3, 2, F, H, C), BF16),
                pltpu.VMEM((3, 2, 2, F, C), F32),
                pltpu.VMEM((3, 2, F + 2, H, C), BF16),
                pltpu.VMEM((3, 2, 2, 2, F, C), F32),
                pltpu.VMEM((2, F + 2, 24, C), F32),
                pltpu.VMEM((2, F, 8, C), F32),
                pltpu.VMEM((C, 128), BF16),
                pltpu.VMEM((128, C), BF16),
                pltpu.VMEM((16, C), F32),
                pltpu.VMEM((16, C), F32),
                pltpu.VMEM((2, 2, 128), F32),
                pltpu.VMEM((4, 2, 128), F32),
                pltpu.VMEM((4, 2, 128), F32),
                pltpu.VMEM((4, n_plane, 2, 128), F32),
                pltpu.VMEM((4, n_line, 2, 128), F32),
                pltpu.SemaphoreType.DMA((4,)),
                pltpu.SemaphoreType.DMA((3, rims)),
                pltpu.SemaphoreType.DMA((3, rims)),
                pltpu.SemaphoreType.DMA((4,)),
                pltpu.SemaphoreType.DMA((4,)),
                pltpu.SemaphoreType.DMA((4,)),
                pltpu.SemaphoreType.DMA((4,)),
            ],
            compiler_params=pltpu.CompilerParams(
                collective_id=0, has_side_effects=True, vmem_limit_bytes=48 << 20
            ),
        )(act, cot, w1.reshape(27, C, C), w2.reshape(27, C, C), b1, g1, o1, g2, o2)

    tile = P(*AXES, None)
    return jax.shard_map(
        step,
        mesh=mesh,
        in_specs=(tile, tile) + (P(),) * 7,
        out_specs=tile,
        check_vma=False,
    )
```

time: 503 us -> 82.3 us (0.16)
  blocking collectives: 312 us -> 0 us
  Pallas kernels: 0 us -> 73.7 us
  other arithmetic: 59.3 us -> 0 us
  starting transfers between devices: 50.7 us -> 0 us
  local copies, waits for them, and re-layouts: 48.4 us -> 8.27 us
  matrix products: 18 us -> 0 us
  waiting for transfers between devices: 8.93 us -> 0 us
    psum x4 -> x0, blocking collectives: 257 us -> none  [the longest x2 130 us: backward_stats(): totals = lax.psum(local_sums, ('row', 'col'))]
    pallas_call x0 -> x1, Pallas kernels: none -> 73.7 us  [step(): pl.pallas_call(functools.partial(kernel, sizes), name='vae_grad', out_sha...]
    all_gather x4 -> x0, blocking collectives: 55.8 us -> none  [prefix_2(): gathered = lax.all_gather(part, axis)]
    ppermute x15 -> x0, starting transfers between devices: 50.7 us -> none  [the longest x6 26.8 us: with_halo(): after = lax.ppermute(first, axis, down)]
    reduce_sum x16 -> x0, other arithmetic: 19.2 us -> none  [the longest x4 6.99 us: backward_stats(): jnp.sum(grad_hat, axis=(1, 2, 4))]
    conv_general_dilated x3 -> x0, matrix products: 18 us -> none  [convolve(): lax.conv_general_dilated(padded[None], kernel, (1, 1, 1), 'VALID', dimens...]
    add x20 -> x0, other arithmetic: 16 us -> none  [the longest x14 13.4 us: add_terms(): return earlier + later]
    conv_general_dilated x10 -> x0, local copies, waits for them, and re-layouts: 11.5 us -> none  [convolve(): lax.conv_general_dilated(padded[None], kernel, (1, 1, 1), 'VALID', dimens...]
  transfers between devices with their start and end apart: 15 -> 0, of which waited for: 4 -> 0; matrix products, arithmetic and copies ran while one was open for 3% -> 0% of each run, Pallas kernels for 0% -> 0%
where the time goes in v1:
time: 82.3 us; the launch traced here: 82 us
  Pallas kernels  73.7 us (90%)
  local copies, waits for them, and re-layouts  8.27 us (10%)
    pallas_call x1, Pallas kernels, step(): pl.pallas_call(functools.partial(kernel, sizes), name='vae_grad', out_sha...  73.7 us
    unnamed x17, local copies, waits for them, and re-layouts  8.27 us

profile of v1, /device:TPU:1, one launch (start us, length us, event | category | flops | bytes accessed | tf_op | source)
XLA Modules:
  0.0 82.0 jit_solution(3646760639475201241)
XLA Ops:
  0.0 0.0 copy-start
  0.0 2.0 %copy-done = bf16[3,3,3,256,256]{4,3,2,1,0:T(8,128)(2,1)S(1)} copy-done((bf16[3,3,3,256,256]{4,3,2,1,0:T(8,128)(2,1)S(1)}, bf16[3,3,3,256,256]{4,3,2,1,0:T(8,128)(2,1)}, u32[]{:S(2)}) %copy-start) | copy-done | bytes 3538968
  2.0 0.0 copy-start.1
  2.0 1.0 %copy-done.1 = bf16[4,16,16,256]{3,2,1,0:T(8,128)(2,1)S(1)} copy-done((bf16[4,16,16,256]{3,2,1,0:T(8,128)(2,1)S(1)}, bf16[4,16,16,256]{3,2,1,0:T(8,128)(2,1)}, u32[]{:S(2)}) %copy-start.1) | copy-done | bytes 524312
  3.0 0.0 copy-start.2
  3.0 1.0 %copy-done.2 = bf16[4,16,16,256]{3,2,1,0:T(8,128)(2,1)S(1)} copy-done((bf16[4,16,16,256]{3,2,1,0:T(8,128)(2,1)S(1)}, bf16[4,16,16,256]{3,2,1,0:T(8,128)(2,1)}, u32[]{:S(2)}) %copy-start.2) | copy-done | bytes 524312
  4.1 0.0 copy-start.3
  4.1 0.7 copy-done.3
  4.8 0.0 copy-start.4
  4.8 0.7 copy-done.4
  5.4 0.0 copy-start.5
  5.4 0.7 copy-done.5
  6.1 0.0 copy-start.6
  6.1 0.7 copy-done.6
  6.8 0.0 copy-start.7
  6.8 0.7 copy-done.7
  7.5 73.7 %vae_grad.1 = bf16[4,16,16,256]{3,2,1,0:T(8,128)(2,1)S(1)} custom-call(bf16[4,16,16,256]{3,2,1,0:T(8,128)(2,1)S(1)} %copy-done.1, bf16[4,16,16,256]{3,2,1,0:T(8,128)(2,1)S(1)} %copy-done.2, bf16[27,256,256]{2,1,0:T(8,128)(2,1)S(1)} %bitcast.2, bf16[27,256,256]{2,1,0:T(8,128)(2,1)} %bitcast.3, f32[256]{0:T(256)S(1)} %copy-done.3, f32[256]{0:T(256)S(1)} %copy-done.4, ...), custom_call_target="tpu_custom_call" | custom-call | tf_op jit(solution)/shard_map/vae_grad/pallas_call | solution.py:572
  81.2 0.8 copy.11
Async XLA Ops:
  0.0 2.0 %copy-start = (bf16[3,3,3,256,256]{4,3,2,1,0:T(8,128)(2,1)S(1)}, bf16[3,3,3,256,256]{4,3,2,1,0:T(8,128)(2,1)}, u32[]{:S(2)}) copy-start(bf16[3,3,3,256,256]{4,3,2,1,0:T(8,128)(2,1)} %param.11) | copy-start | bytes 10616836
  2.0 1.0 %copy-start.1 = (bf16[4,16,16,256]{3,2,1,0:T(8,128)(2,1)S(1)}, bf16[4,16,16,256]{3,2,1,0:T(8,128)(2,1)}, u32[]{:S(2)}) copy-start(bf16[4,16,16,256]{3,2,1,0:T(8,128)(2,1)} %act_hbm.1) | copy-start | bytes 1572868
  3.0 1.0 %copy-start.2 = (bf16[4,16,16,256]{3,2,1,0:T(8,128)(2,1)S(1)}, bf16[4,16,16,256]{3,2,1,0:T(8,128)(2,1)}, u32[]{:S(2)}) copy-start(bf16[4,16,16,256]{3,2,1,0:T(8,128)(2,1)} %cot_hbm.1) | copy-start | bytes 1572868
  4.1 0.7 copy-start.3
  4.8 0.7 copy-start.4
  5.4 0.7 copy-start.5
  6.1 0.7 copy-start.6
  6.8 0.7 copy-start.7

commit v2 on v1

--- a/solution.py
+++ b/solution.py
@@ -83,20 +83,26 @@
     cot_hbm,
     w1_hbm,
     w2_hbm,
-    bias1,
-    gain1,
-    offset1,
-    gain2,
-    offset2,
+    bias1_hbm,
+    gain1_hbm,
+    offset1_hbm,
+    gain2_hbm,
+    offset2_hbm,
     out_ref,
     actf,
     cotf,
     gmf,
     w1,
     w2,
+    bias1,
+    gain1,
+    offset1,
+    gain2,
+    offset2,
     taps,
     grad,
-    lay,
+    layf,
+    xf,
     stage,
     colpack,
     cornerpack,
@@ -108,6 +114,8 @@
     spread_m,
     stat1,
     stat2,
+    rest1,
+    rest2,
     ends,
     mine,
     line_mine,
@@ -142,6 +150,11 @@
         pltpu.make_async_copy(cot_hbm, cotf.at[pl.ds(0, F), pl.ds(1, H)], in_sem.at[1]),
         pltpu.make_async_copy(w1_hbm, w1, in_sem.at[2]),
         pltpu.make_async_copy(w2_hbm, w2, in_sem.at[3]),
+        pltpu.make_async_copy(bias1_hbm, bias1, in_sem.at[4]),
+        pltpu.make_async_copy(gain1_hbm, gain1, in_sem.at[5]),
+        pltpu.make_async_copy(offset1_hbm, offset1, in_sem.at[6]),
+        pltpu.make_async_copy(gain2_hbm, gain2, in_sem.at[7]),
+        pltpu.make_async_copy(offset2_hbm, offset2, in_sem.at[8]),
     ]
     for load in loads:
         load.start()
@@ -211,18 +224,23 @@
         mean = prefix[0:1] / n
         return mean, lax.rsqrt(prefix[1:2] / n - mean * mean + EPS)
 
-    def spread(first, second, before=None):
+    def spread(first, second, before=None, after=None):
         row = lax.broadcasted_iota(jnp.int32, (8, 128), 0)
         f = frame_of_lane((8, 128))
         halves = []
         for i, own in enumerate((first, second)):
             own = jnp.broadcast_to(own, (8, 128))
-            if before is None:
-                halves.append(jnp.where(f == row, own, 0.0))
-            else:
+            if before is not None:
                 ahead = jnp.broadcast_to(before[i], (8, 128))
                 frame = jnp.where(row < 2, row + 2, row - 2)
-                halves.append(jnp.where(f == frame, jnp.where(row < 2, ahead, own), 0.0))
+                own = jnp.where(row < 2, ahead, own)
+            elif after is not None:
+                behind = jnp.broadcast_to(after[i], (8, 128))
+                frame = jnp.where(row < F, row, row - F)
+                own = jnp.where(row < F, own, behind)
+            else:
+                frame = row
+            halves.append(jnp.where(f == frame, own, 0.0))
         return exact_dot(jnp.concatenate(halves, axis=0), spread_m[...])
 
     def forward_end(k, layer):
@@ -252,11 +270,13 @@
     def backward_end(k):
         got = line_end(k)
         zero = jnp.zeros((2, 128), F32)
-        later = zero
-        for j in range(len(line)):
-            later = later + jnp.where(t < j + 1, got[j], zero)
-        rest = over_frames(later) + running_back(line_mine[k])
-        return spread(rest[0:1], rest[1:2])
+        near = jnp.where(t < tms - 1, got[-1], zero)
+        far = zero
+        for j in range(len(line) - 1):
+            far = far + jnp.where(t < j + 1, got[j], zero)
+        rest = over_frames(far + near) + running_back(line_mine[k])
+        behind = over_frames(far) + running_back(near)
+        return spread(rest[0:1], rest[1:2], after=(behind[0:1], behind[1:2]))
 
     def put_stage(start, x):
         for i in range(2):
@@ -304,22 +324,23 @@
             for j, (o, src, dst) in enumerate(moves)
         ]
 
-    def side_columns(k, own, halo, turn, change):
+    def side_columns(ks, own, halo, turn, change):
         inner = F - 2 if turn > 0 else 0
         for side in range(2):
 
             def one(f, carry, side=side):
-                colside[side, f, pl.ds(1, H)] = change(colhalo[k, side, f].astype(F32), f)
+                values = [colhalo[k, side, f].astype(F32) for k in ks]
+                colside[side, f, pl.ds(1, H)] = change(f, *values)
                 return carry
 
             lax.fori_loop(0, F + 2, one, 0)
             for end, place in ((0, 0), (1, H + 1)):
                 for f in range(F):
-                    value = cornerhalo[k, 0, end, side, pl.ds(f, 1)]
-                    colside[side, own + f, pl.ds(place, 1)] = change(value, own + f)
+                    values = [cornerhalo[k, 0, end, side, pl.ds(f, 1)] for k in ks]
+                    colside[side, own + f, pl.ds(place, 1)] = change(own + f, *values)
                 for f in range(2):
-                    value = cornerhalo[k, 1, end, side, pl.ds(inner + f, 1)]
-                    colside[side, halo + f, pl.ds(place, 1)] = change(value, halo + f)
+                    values = [cornerhalo[k, 1, end, side, pl.ds(inner + f, 1)] for k in ks]
+                    colside[side, halo + f, pl.ds(place, 1)] = change(halo + f, *values)
 
         @pl.when(c == 0)
         def _():
@@ -334,7 +355,7 @@
 
         def one(f, carry):
             for h in range(0, H + 2, 6):
-                x = change(full[f, pl.ds(h, 6)].astype(F32), f)
+                x = change(f, full[f, pl.ds(h, 6)].astype(F32))
                 left = colside[0, f, pl.ds(h, 6)].reshape(6, 1, C)
                 right = colside[1, f, pl.ds(h, 6)].reshape(6, 1, C)
                 taps[1, f, pl.ds(h, 6)] = x.astype(BF16)
@@ -388,6 +409,8 @@
         e = d * s * (1.0 + pre * (1.0 - s)) * gain
         return e, sums(e), sums(e * normed)
 
+    for load in loads[4:]:
+        load.wait()
     vectors = [ref[...].reshape(1, C) for ref in (bias1, gain1, offset1, gain2, offset2)]
     bias1, gain1, offset1, gain2, offset2 = vectors
 
@@ -424,14 +447,14 @@
     for copy in past:
         copy.wait_recv()
 
-    def activate(x, f):
+    def activate(f, x):
         shape = (1,) * (x.ndim - 1) + (C,)
         mean = row_of(stat1, f).reshape(shape)
         inverse = row_of(stat1, f + 8).reshape(shape)
         u = (x - mean) * inverse * gain1.reshape(shape) + offset1.reshape(shape)
         return u * sigmoid(u)
 
-    side_columns(0, 2, 0, 1, activate)
+    side_columns((0,), 2, 0, 1, activate)
     build(actf, 0, 0, activate)
     loads[2].wait()
 
@@ -440,8 +463,9 @@
         hidden = convolve(f, w1, False)
         x = actf[pl.ds(f + 2, 2), pl.ds(1, H)].astype(F32).reshape(2 * H * W, C)
         y = (x + hidden + bias1).astype(BF16)
-        lay[pl.ds(f, 2)] = y.reshape(2, H, W, C)
+        layf[pl.ds(f, 2), pl.ds(1, H)] = y.reshape(2, H, W, C)
         y = y.astype(F32)
+        put_stage(f * H * W, y)
         for j in range(2):
             z = y[j * H * W : (j + 1) * H * W]
             part[0, f + j] = sums(z)
@@ -450,12 +474,16 @@
 
     lax.fori_loop(0, F // 2, first_layer, 0)
     plane_start(1)
+    pack_rims(2)
+    layer_rims = rim_copies(2, layf, 0, 4, -1)
+    for copy in layer_rims:
+        copy.start()
 
     for copy in future:
         copy.wait_recv()
     loads[3].wait()
-    same = lambda x, f: x
-    side_columns(1, 0, 4, -1, same)
+    same = lambda f, x: x
+    side_columns((1,), 0, 4, -1, same)
     build(cotf, 4, tms - 1, same)
 
     def second_grad(f):
@@ -470,10 +498,13 @@
         mean, inverse = row_of(stat2, f), row_of(stat2, f + 8)
         a = b = jnp.zeros((8, C), F32)
         for h in range(0, H, 8):
-            v = lay[f, pl.ds(h, 8)].astype(F32).reshape(8 * W, C)
+            v = layf[f, pl.ds(h + 1, 8)].astype(F32).reshape(8 * W, C)
             d = grad[f, pl.ds(h, 8)].reshape(8 * W, C)
             e, da, db = norm_grad(v, d, mean, inverse, gain2, offset2)
-            grad[f, pl.ds(h, 8)] = e.reshape(8, W, C)
+            x = cotf[f, pl.ds(h + 1, 8)].astype(F32).reshape(8 * W, C) + inverse * e
+            grad[f, pl.ds(h, 8)] = x.reshape(8, W, C)
+            put_stage(f * H * W + h * W, x)
+            xf[f, pl.ds(h + 1, 8)] = x.astype(BF16).reshape(8, W, C)
             a, b = a + da, b + db
         part[0, f] = a
         part[1, f] = b
@@ -481,35 +512,47 @@
 
     lax.fori_loop(0, F, second_norm, 0)
     plane_start(2)
+    pack_rims(3)
+    x_rims = rim_copies(3, xf, 0, 4, -1)
+    for copy in x_rims:
+        copy.start()
     line_start(2, backward_terms(2, 1))
-    rest2 = backward_end(2)
-    ends_rows = stat2[8:16]
-    stat2[0:8] = ends_rows
-    part[0, 0] = rest2[0:8]
-    part[0, 1] = rest2[8:16]
+    rest2[...] = backward_end(2)
+
+    def settle(f, x, v):
+        shape = (1,) * (x.ndim - 1) + (C,)
+        r1 = row_of(rest2, f).reshape(shape)
+        r2 = row_of(rest2, f + 8).reshape(shape)
+        return x + (r1 + 2.0 * v * r2)
 
     def middle(f, carry):
-        inverse = row_of(stat2, f)
-        r1 = part[0, 0, pl.ds(f, 1)]
-        r2 = part[0, 1, pl.ds(f, 1)]
         for h in range(0, H, 8):
-            v = lay[f, pl.ds(h, 8)].astype(F32).reshape(8 * W, C)
-            e = grad[f, pl.ds(h, 8)].reshape(8 * W, C)
-            x = cotf[f, pl.ds(h + 1, 8)].astype(F32).reshape(8 * W, C)
-            y = (x + (inverse * e + r1 + 2.0 * v * r2)).astype(BF16)
-            gmf[f, pl.ds(h + 1, 8)] = y.reshape(8, W, C)
-            put_stage(f * H * W + h * W, y.astype(F32))
+            v = layf[f, pl.ds(h + 1, 8)].astype(F32)
+            gmf[f, pl.ds(h + 1, 8)] = settle(f, grad[f, pl.ds(h, 8)], v).astype(BF16)
         return carry
 
     lax.fori_loop(0, F, middle, 0)
-    pack_rims(2)
-    middle_rims = rim_copies(2, gmf, 0, 4, -1)
-    for copy in middle_rims:
-        copy.start()
-    for copy in middle_rims:
+    for copy in layer_rims + x_rims:
         copy.wait_recv()
 
-    side_columns(2, 0, 4, -1, same)
+    def settle_rows(f, h, n):
+        x, v = xf[f, pl.ds(h, n)].astype(F32), layf[f, pl.ds(h, n)].astype(F32)
+        gmf[f, pl.ds(h, n)] = settle(f, x, v).astype(BF16)
+
+    def middle_rows(f, carry):
+        settle_rows(f, 0, 1)
+        settle_rows(f, H + 1, 1)
+        return carry
+
+    def middle_frames(f, carry):
+        for h in range(0, H + 2, 6):
+            settle_rows(f, h, 6)
+        return carry
+
+    lax.fori_loop(0, F, middle_rows, 0)
+    lax.fori_loop(F, F + 2, middle_frames, 0)
+    side_columns((3, 2), 0, 4, -1, settle)
+
     build(gmf, 4, tms - 1, same)
 
     def first_grad(i, carry):
@@ -535,14 +578,11 @@
     lax.fori_loop(0, F, first_norm, 0)
     plane_start(3)
     line_start(3, backward_terms(3, 0))
-    rest1 = backward_end(3)
-    part[0, 0] = rest1[0:8]
-    part[0, 1] = rest1[8:16]
+    rest1[...] = backward_end(3)
 
     def finish(f, carry):
         inverse = row_of(stat1, f + 10)
-        r1 = part[0, 0, pl.ds(f, 1)]
-        r2 = part[0, 1, pl.ds(f, 1)]
+        r1, r2 = row_of(rest1, f), row_of(rest1, f + 8)
         for h in range(0, H, 8):
             v = actf[f + 2, pl.ds(h + 1, 8)].astype(F32).reshape(8 * W, C)
             e = grad[f, pl.ds(h, 8)].reshape(8 * W, C)
@@ -553,7 +593,7 @@
 
     lax.fori_loop(0, F, finish, 0)
 
-    for copy in past + future + middle_rims:
+    for copy in past + future + layer_rims + x_rims:
         copy.wait_send()
     for k in range(4):
         await_all(plane_in.at[k], plane_send.at[k])
@@ -567,13 +607,15 @@
     full = (F + 2, H + 2, W, C)
 
     def step(act, cot, w1, b1, g1, o1, w2, g2, o2):
-        hbm = pl.BlockSpec(memory_space=pl.ANY)
+        hbm = pl.BlockSpec(memory_space=pltpu.HBM)
+        operands = (act, cot, w1.reshape(27, C, C), w2.reshape(27, C, C), b1, g1, o1, g2, o2)
+        operands = [pltpu.with_memory_space_constraint(x, pltpu.HBM) for x in operands]
         vmem = pl.BlockSpec(memory_space=pltpu.VMEM)
         return pl.pallas_call(
             functools.partial(kernel, sizes),
             name="vae_grad",
-            out_shape=jax.ShapeDtypeStruct((F, H, W, C), BF16),
-            in_specs=[hbm] * 4 + [vmem] * 5,
+            out_shape=pltpu.VMEM((F, H, W, C), BF16),
+            in_specs=[hbm] * 9,
             out_specs=vmem,
             scratch_shapes=[
                 pltpu.VMEM(full, BF16),
@@ -581,18 +623,26 @@
                 pltpu.VMEM(full, BF16),
                 pltpu.VMEM((27, C, C), BF16),
                 pltpu.VMEM((27, C, C), BF16),
+                pltpu.VMEM((C,), F32),
+                pltpu.VMEM((C,), F32),
+                pltpu.VMEM((C,), F32),
+                pltpu.VMEM((C,), F32),
+                pltpu.VMEM((C,), F32),
                 pltpu.VMEM((3,) + full, BF16),
                 pltpu.VMEM((F, H, W, C), F32),
-                pltpu.VMEM((F, H, W, C), BF16),
+                pltpu.VMEM(full, BF16),
+                pltpu.VMEM(full, BF16),
                 pltpu.VMEM((2, F * H * W, 128), F32),
-                pltpu.VMEM((3, 2, F, H, C), BF16),
-                pltpu.VMEM((3, 2, 2, F, C), F32),
-                pltpu.VMEM((3, 2, F + 2, H, C), BF16),
-                pltpu.VMEM((3, 2, 2, 2, F, C), F32),
+                pltpu.VMEM((4, 2, F, H, C), BF16),
+                pltpu.VMEM((4, 2, 2, F, C), F32),
+                pltpu.VMEM((4, 2, F + 2, H, C), BF16),
+                pltpu.VMEM((4, 2, 2, 2, F, C), F32),
                 pltpu.VMEM((2, F + 2, 24, C), F32),
                 pltpu.VMEM((2, F, 8, C), F32),
                 pltpu.VMEM((C, 128), BF16),
                 pltpu.VMEM((128, C), BF16),
+                pltpu.VMEM((16, C), F32),
+                pltpu.VMEM((16, C), F32),
                 pltpu.VMEM((16, C), F32),
                 pltpu.VMEM((16, C), F32),
                 pltpu.VMEM((2, 2, 128), F32),
@@ -600,18 +650,18 @@
                 pltpu.VMEM((4, 2, 128), F32),
                 pltpu.VMEM((4, n_plane, 2, 128), F32),
                 pltpu.VMEM((4, n_line, 2, 128), F32),
-                pltpu.SemaphoreType.DMA((4,)),
-                pltpu.SemaphoreType.DMA((3, rims)),
-                pltpu.SemaphoreType.DMA((3, rims)),
+                pltpu.SemaphoreType.DMA((9,)),
+                pltpu.SemaphoreType.DMA((4, rims)),
+                pltpu.SemaphoreType.DMA((4, rims)),
                 pltpu.SemaphoreType.DMA((4,)),
                 pltpu.SemaphoreType.DMA((4,)),
                 pltpu.SemaphoreType.DMA((4,)),
                 pltpu.SemaphoreType.DMA((4,)),
             ],
             compiler_params=pltpu.CompilerParams(
-                collective_id=0, has_side_effects=True, vmem_limit_bytes=48 << 20
+                collective_id=0, has_side_effects=True, vmem_limit_bytes=62 << 20
             ),
-        )(act, cot, w1.reshape(27, C, C), w2.reshape(27, C, C), b1, g1, o1, g2, o2)
+        )(*operands)
 
     tile = P(*AXES, None)
     return jax.shard_map(

time: 82.3 us -> 69.1 us (0.84)
  local copies, waits for them, and re-layouts: 8.27 us -> 0.8 us
  Pallas kernels: 73.7 us -> 68.2 us
    unnamed x17 -> x1, local copies, waits for them, and re-layouts: 8.27 us -> 0.8 us
    pallas_call x1, Pallas kernels: 73.7 us -> 68.2 us  [step(): pl.pallas_call(functools.partial(kernel, sizes), name='vae_grad', out_sha...]
where the time goes in v2:
time: 69.1 us; the launch traced here: 69 us
  Pallas kernels  68.2 us (99%)
  local copies, waits for them, and re-layouts  0.8 us (1%)
    pallas_call x1, Pallas kernels, step(): pl.pallas_call(functools.partial(kernel, sizes), name='vae_grad', out_sha...  68.2 us

profile of v2, /device:TPU:1, one launch (start us, length us, event | category | flops | bytes accessed | tf_op | source)
XLA Modules:
  0.0 69.0 jit_solution(13984952145648248044)
XLA Ops:
  0.0 68.2 %vae_grad.1 = bf16[4,16,16,256]{3,2,1,0:T(8,128)(2,1)S(1)} custom-call(bf16[4,16,16,256]{3,2,1,0:T(8,128)(2,1)} %act_hbm.1, bf16[4,16,16,256]{3,2,1,0:T(8,128)(2,1)} %cot_hbm.1, bf16[27,256,256]{2,1,0:T(8,128)(2,1)} %bitcast.2, bf16[27,256,256]{2,1,0:T(8,128)(2,1)} %bitcast.3, f32[256]{0:T(256)} %bias1_hbm.1, f32[256]{0:T(256)} %gain1_hbm.1, ...), custom_call_target="tpu_custom_call" | custom-call | tf_op jit(solution)/shard_map/vae_grad/pallas_call | solution.py:614
  68.2 0.8 %copy.11 = bf16[4,16,16,256]{3,2,1,0:T(8,128)(2,1)} copy(bf16[4,16,16,256]{3,2,1,0:T(8,128)(2,1)S(1)} %vae_grad.1) | data formatting | bytes 1048576

commit v3 on v2

--- a/solution.py
+++ b/solution.py
@@ -14,6 +14,7 @@
 F, H, W, C, G = 4, 16, 16, 256, 32
 TAPS = tuple(itertools.product(range(3), repeat=3))
 AXES = ("tm", "row", "col")
+PIECES = ((1, 6), (7, 10))
 
 
 def offsets_of(sizes):
@@ -21,6 +22,7 @@
     plane = [(0, b, d) for b in range(rows) for d in range(cols) if (b, d) != (0, 0)]
     plane.sort(key=lambda o: -(min(o[1], rows - o[1]) + min(o[2], cols - o[2])))
     line = [(a, 0, 0) for a in range(1, tms)]
+    line.sort(key=lambda o: -min(o[0], tms - o[0]))
     rims = [
         (a % tms, b % rows, d % cols)
         for a in (-1, 1)
@@ -28,7 +30,17 @@
         for d in (-1, 0, 1)
     ]
     everyone = list(dict.fromkeys(plane + line + rims))
-    return plane, line, everyone
+    chips = [
+        (a, b, d)
+        for a in range(tms)
+        for b in range(rows)
+        for d in range(0, cols, 2)
+        if (a, b, d) != (0, 0, 0)
+    ]
+    chips.sort(
+        key=lambda o: -2 * (min(o[0], tms - o[0]) + min(o[1], rows - o[1])) - min(o[2], cols - o[2])
+    )
+    return plane, line, everyone, chips
 
 
 def sigmoid(u):
@@ -121,6 +133,11 @@
     line_mine,
     plane_in,
     line_in,
+    chip_mine,
+    chip_brief,
+    pair_in,
+    near_in,
+    far_in,
     in_sem,
     halo_send,
     halo_recv,
@@ -128,10 +145,16 @@
     plane_recv,
     line_send,
     line_recv,
+    pair_send,
+    pair_recv,
+    near_send,
+    near_recv,
+    far_send,
+    far_recv,
 ):
     tms, rows, cols = sizes
     t, r, c = (lax.axis_index(a) for a in AXES)
-    plane, line, everyone = offsets_of(sizes)
+    plane, line, everyone, chips = offsets_of(sizes)
     plane_cells = float(H * rows * W * cols * (C // G))
 
     def at(o):
@@ -188,7 +211,7 @@
     def line_copy(k, j):
         return pltpu.make_async_remote_copy(
             src_ref=line_mine.at[k],
-            dst_ref=line_in.at[k, j],
+            dst_ref=line_in.at[k, line[j][0] - 1],
             send_sem=line_send.at[k],
             recv_sem=line_recv.at[k],
             device_id=at(line[j]),
@@ -199,7 +222,6 @@
         pltpu.make_async_copy(buffer, buffer, sem).wait()
 
     def plane_start(k):
-        mine[k] = packed_sums()
         for j in range(len(plane)):
             plane_copy(k, j).start()
 
@@ -243,23 +265,79 @@
             halves.append(jnp.where(f == frame, own, 0.0))
         return exact_dot(jnp.concatenate(halves, axis=0), spread_m[...])
 
-    def forward_end(k, layer):
-        got = line_end(k)
+    def first_end():
+        got = line_end(0)
         zero = jnp.zeros((2, 128), F32)
         near = jnp.where(t >= 1, got[0], zero)
         far = zero
         for j in range(1, len(line)):
             far = far + jnp.where(t >= j + 1, got[j], zero)
-        own = moments(over_frames(far + near) + running(line_mine[k]), counts(t * F))
+        own = moments(over_frames(far + near) + running(line_mine[0]), counts(t * F))
+        ends[0, 0:1] = own[0]
+        ends[0, 1:2] = own[1]
+        before = moments(over_frames(far) + running(near), counts(t * F - F))
+        return spread(own[0], own[1], before)
+
+    def partner_copy(k):
+        return pltpu.make_async_remote_copy(
+            src_ref=mine.at[k],
+            dst_ref=pair_in.at[k],
+            send_sem=pair_send.at[k],
+            recv_sem=pair_recv.at[k],
+            device_id=(t, r, c + 1 - 2 * lax.rem(c, 2)),
+            device_id_type=MESH,
+        )
+
+    def chip_copy(k, o):
+        inside = o[0] == 0
+        place = o[1] * (cols // 2) + o[2] // 2
+        return pltpu.make_async_remote_copy(
+            src_ref=chip_mine.at[k] if inside else chip_brief.at[k],
+            dst_ref=near_in.at[k, place - 1] if inside else far_in.at[k, o[0] - 1, place],
+            send_sem=(near_send if inside else far_send).at[k],
+            recv_sem=(near_recv if inside else far_recv).at[k],
+            device_id=at(o),
+            device_id_type=MESH,
+        )
+
+    def chip_start(k, value):
+        mine[k] = value
+        pair = partner_copy(k)
+        pair.start()
+        pair.wait_recv()
+        value = value + pair_in[k]
+        chip_mine[k] = value
+        f = frame_of_lane((1, 128))
+        whole = over_frames(value)
+        first = jnp.where(f == 2, pltpu.roll(value, 64, 1)[0:1], pltpu.roll(value, 96, 1)[1:2])
+        both = jnp.where(f == 0, whole[0:1], whole[1:2])
+        chip_brief[k] = jnp.where(f < 2, both, first)
+        for o in chips:
+            chip_copy(k, o).start()
+        pair.wait_send()
+
+    def chip_end(k):
+        await_all(near_in.at[k], near_recv.at[k])
+        own = chip_mine[k] + jnp.sum(near_in[k], axis=0)
+        await_all(far_in.at[k], far_recv.at[k])
+        return own, [jnp.sum(far_in[k, a], axis=0) for a in range(tms - 1)]
+
+    def widen(x):
+        f = frame_of_lane((1, 128))
+        rows = [jnp.where(f == i, x, 0.0) for i in range(2)]
+        return over_frames(jnp.concatenate(rows, axis=0))
+
+    def forward_end(k, layer):
+        own, got = chip_end(k)
+        earlier = jnp.zeros((1, 128), F32)
+        for j in range(tms - 1):
+            earlier = earlier + jnp.where(t >= j + 1, got[j], 0.0)
+        own = moments(widen(earlier) + running(own), counts(t * F))
         ends[layer, 0:1] = own[0]
         ends[layer, 1:2] = own[1]
-        before = None
-        if layer == 0:
-            before = moments(over_frames(far) + running(near), counts(t * F - F))
-        return spread(own[0], own[1], before)
-
-    def backward_terms(k, layer):
-        totals = plane_end(k)
+        return spread(own[0], own[1])
+
+    def backward_terms(totals, layer):
         mean, inverse = ends[layer, 0:1], ends[layer, 1:2]
         n = counts(t * F)
         a, b = totals[0:1], totals[1:2]
@@ -268,19 +346,28 @@
         return jnp.concatenate([first, second], axis=0)
 
     def backward_end(k):
-        got = line_end(k)
-        zero = jnp.zeros((2, 128), F32)
-        near = jnp.where(t < tms - 1, got[-1], zero)
-        far = zero
-        for j in range(len(line) - 1):
-            far = far + jnp.where(t < j + 1, got[j], zero)
-        rest = over_frames(far + near) + running_back(line_mine[k])
-        behind = over_frames(far) + running_back(near)
+        own, got = chip_end(k)
+        near = jnp.where(t < tms - 1, got[-1], 0.0)
+        later = near
+        for j in range(tms - 2):
+            later = later + jnp.where(t < j + 1, got[j], 0.0)
+        later = widen(later)
+        f = frame_of_lane((1, 128))
+        first = jnp.concatenate([pltpu.roll(near, 96, 1), pltpu.roll(near, 64, 1)], axis=0)
+        behind = later - jnp.where(f == 1, first, 0.0)
+        rest = later + running_back(own)
         return spread(rest[0:1], rest[1:2], after=(behind[0:1], behind[1:2]))
 
     def put_stage(start, x):
         for i in range(2):
             stage[i, pl.ds(start, x.shape[0])] = x[:, i * 128 : i * 128 + 128]
+
+    def fill_stage(full):
+        def one(f, carry):
+            put_stage(f * H * W, full[f, pl.ds(1, H)].astype(F32).reshape(H * W, C))
+            return carry
+
+        lax.fori_loop(0, F, one, 0)
 
     def staged(start, size, stride):
         return jnp.concatenate(
@@ -298,7 +385,10 @@
     def rim_copies(k, full, own, halo, turn):
         last = own + (F - 2 if turn > 0 else 0)
         inner = F - 2 if turn > 0 else 0
-        moves = [((turn, 0, 0), full.at[pl.ds(last, 2), pl.ds(1, H)], full.at[pl.ds(halo, 2), pl.ds(1, H)])]
+        moves = []
+        for start, n in PIECES:
+            src = full.at[pl.ds(last, 2), pl.ds(start, n)]
+            moves.append(((turn, 0, 0), src, full.at[pl.ds(halo, 2), pl.ds(start, n)]))
         for step, src, dst in ((1, H, 0), (-1, 1, H + 1)):
             moves.append(((0, step, 0), full.at[pl.ds(own, F), src], full.at[pl.ds(own, F), dst]))
             moves.append(((turn, step, 0), full.at[pl.ds(last, 2), src], full.at[pl.ds(halo, 2), dst]))
@@ -424,25 +514,24 @@
         return carry
 
     lax.fori_loop(0, F, first_sums, 0)
-    pack_rims(0)
+    mine[0] = packed_sums()
     pl.semaphore_wait(barrier, len(everyone))
     plane_start(0)
     past = rim_copies(0, actf, 2, 0, 1)
-    for copy in past:
+    for copy in past[1:6]:
+        copy.start()
+    pack_rims(0)
+    for copy in past[6:]:
         copy.start()
     loads[1].wait()
-
-    def to_stage(f, carry):
-        put_stage(f * H * W, cotf[f, pl.ds(1, H)].astype(F32).reshape(H * W, C))
-        return carry
-
-    lax.fori_loop(0, F, to_stage, 0)
+    fill_stage(cotf)
     pack_rims(1)
+    line_start(0, plane_end(0))
+    past[0].start()
     future = rim_copies(1, cotf, 0, 4, -1)
     for copy in future:
         copy.start()
-    line_start(0, plane_end(0))
-    stat1[...] = forward_end(0, 0)
+    stat1[...] = first_end()
 
     for copy in past:
         copy.wait_recv()
@@ -465,7 +554,6 @@
         y = (x + hidden + bias1).astype(BF16)
         layf[pl.ds(f, 2), pl.ds(1, H)] = y.reshape(2, H, W, C)
         y = y.astype(F32)
-        put_stage(f * H * W, y)
         for j in range(2):
             z = y[j * H * W : (j + 1) * H * W]
             part[0, f + j] = sums(z)
@@ -473,10 +561,13 @@
         return carry
 
     lax.fori_loop(0, F // 2, first_layer, 0)
-    plane_start(1)
+    chip_start(1, packed_sums())
+    layer_rims = rim_copies(2, layf, 0, 4, -1)
+    for copy in layer_rims[:6]:
+        copy.start()
+    fill_stage(layf)
     pack_rims(2)
-    layer_rims = rim_copies(2, layf, 0, 4, -1)
-    for copy in layer_rims:
+    for copy in layer_rims[6:]:
         copy.start()
 
     for copy in future:
@@ -490,7 +581,6 @@
         grad[pl.ds(f, 2)] = convolve(f, w2, True).reshape(2, H, W, C)
 
     second_grad(0)
-    line_start(1, plane_end(1))
     second_grad(2)
     stat2[...] = forward_end(1, 1)
 
@@ -503,7 +593,6 @@
             e, da, db = norm_grad(v, d, mean, inverse, gain2, offset2)
             x = cotf[f, pl.ds(h + 1, 8)].astype(F32).reshape(8 * W, C) + inverse * e
             grad[f, pl.ds(h, 8)] = x.reshape(8, W, C)
-            put_stage(f * H * W + h * W, x)
             xf[f, pl.ds(h + 1, 8)] = x.astype(BF16).reshape(8, W, C)
             a, b = a + da, b + db
         part[0, f] = a
@@ -511,12 +600,14 @@
         return carry
 
     lax.fori_loop(0, F, second_norm, 0)
-    plane_start(2)
+    chip_start(2, backward_terms(packed_sums(), 1))
+    x_rims = rim_copies(3, xf, 0, 4, -1)
+    for copy in x_rims[:6]:
+        copy.start()
+    fill_stage(xf)
     pack_rims(3)
-    x_rims = rim_copies(3, xf, 0, 4, -1)
-    for copy in x_rims:
+    for copy in x_rims[6:]:
         copy.start()
-    line_start(2, backward_terms(2, 1))
     rest2[...] = backward_end(2)
 
     def settle(f, x, v):
@@ -576,8 +667,7 @@
         return carry
 
     lax.fori_loop(0, F, first_norm, 0)
-    plane_start(3)
-    line_start(3, backward_terms(3, 0))
+    chip_start(3, backward_terms(packed_sums(), 0))
     rest1[...] = backward_end(3)
 
     def finish(f, carry):
@@ -595,15 +685,18 @@
 
     for copy in past + future + layer_rims + x_rims:
         copy.wait_send()
-    for k in range(4):
-        await_all(plane_in.at[k], plane_send.at[k])
-        await_all(line_in.at[k], line_send.at[k])
+    await_all(plane_in.at[0], plane_send.at[0])
+    await_all(line_in.at[0], line_send.at[0])
+    for k in range(1, 4):
+        await_all(near_in.at[k], near_send.at[k])
+        await_all(far_in.at[k], far_send.at[k])
 
 
 def solution(mesh):
     sizes = tuple(mesh.shape[a] for a in AXES)
     n_plane, n_line = sizes[1] * sizes[2] - 1, sizes[0] - 1
-    rims = 17
+    n_chips = sizes[1] * sizes[2] // 2
+    rims = 18
     full = (F + 2, H + 2, W, C)
 
     def step(act, cot, w1, b1, g1, o1, w2, g2, o2):
@@ -648,15 +741,17 @@
                 pltpu.VMEM((2, 2, 128), F32),
                 pltpu.VMEM((4, 2, 128), F32),
                 pltpu.VMEM((4, 2, 128), F32),
-                pltpu.VMEM((4, n_plane, 2, 128), F32),
-                pltpu.VMEM((4, n_line, 2, 128), F32),
+                pltpu.VMEM((1, n_plane, 2, 128), F32),
+                pltpu.VMEM((1, n_line, 2, 128), F32),
+                pltpu.VMEM((4, 2, 128), F32),
+                pltpu.VMEM((4, 1, 128), F32),
+                pltpu.VMEM((4, 2, 128), F32),
+                pltpu.VMEM((4, n_chips - 1, 2, 128), F32),
+                pltpu.VMEM((4, n_line, n_chips, 1, 128), F32),
                 pltpu.SemaphoreType.DMA((9,)),
                 pltpu.SemaphoreType.DMA((4, rims)),
                 pltpu.SemaphoreType.DMA((4, rims)),
-                pltpu.SemaphoreType.DMA((4,)),
-                pltpu.SemaphoreType.DMA((4,)),
-                pltpu.SemaphoreType.DMA((4,)),
-                pltpu.SemaphoreType.DMA((4,)),
+                *[pltpu.SemaphoreType.DMA((4,))] * 10,
             ],
             compiler_params=pltpu.CompilerParams(
                 collective_id=0, has_side_effects=True, vmem_limit_bytes=62 << 20

time: 69.1 us -> 65.5 us (0.948)
  Pallas kernels: 68.2 us -> 64.6 us
    pallas_call x1, Pallas kernels: 68.2 us -> 64.6 us  [step(): pl.pallas_call(functools.partial(kernel, sizes), name='vae_grad', out_sha...]
where the time goes in v3:
time: 65.5 us; the launch traced here: 65.4 us
  Pallas kernels  64.6 us (99%)
  local copies, waits for them, and re-layouts  0.8 us (1%)
    pallas_call x1, Pallas kernels, step(): pl.pallas_call(functools.partial(kernel, sizes), name='vae_grad', out_sha...  64.6 us

profile of v3, /device:TPU:1, one launch (start us, length us, event | category | flops | bytes accessed | tf_op | source)
XLA Modules:
  0.0 65.4 jit_solution(6792505353422763671)
XLA Ops:
  0.0 64.6 %vae_grad.1 = bf16[4,16,16,256]{3,2,1,0:T(8,128)(2,1)S(1)} custom-call(bf16[4,16,16,256]{3,2,1,0:T(8,128)(2,1)} %act_hbm.1, bf16[4,16,16,256]{3,2,1,0:T(8,128)(2,1)} %cot_hbm.1, bf16[27,256,256]{2,1,0:T(8,128)(2,1)} %bitcast.2, bf16[27,256,256]{2,1,0:T(8,128)(2,1)} %bitcast.3, f32[256]{0:T(256)} %bias1_hbm.1, f32[256]{0:T(256)} %gain1_hbm.1, ...), custom_call_target="tpu_custom_call" | custom-call | tf_op jit(solution)/shard_map/vae_grad/pallas_call | solution.py:707
  64.6 0.8 %copy.11 = bf16[4,16,16,256]{3,2,1,0:T(8,128)(2,1)} copy(bf16[4,16,16,256]{3,2,1,0:T(8,128)(2,1)S(1)} %vae_grad.1) | data formatting | bytes 1048576

commit v4 on v3

--- a/solution.py
+++ b/solution.py
@@ -138,6 +138,7 @@
     pair_in,
     near_in,
     far_in,
+    arrived,
     in_sem,
     halo_send,
     halo_recv,
@@ -294,13 +295,21 @@
         return pltpu.make_async_remote_copy(
             src_ref=chip_mine.at[k] if inside else chip_brief.at[k],
             dst_ref=near_in.at[k, place - 1] if inside else far_in.at[k, o[0] - 1, place],
-            send_sem=(near_send if inside else far_send).at[k],
-            recv_sem=(near_recv if inside else far_recv).at[k],
+            send_sem=near_send.at[k] if inside else far_send.at[k, o[0] - 1],
+            recv_sem=near_recv.at[k] if inside else far_recv.at[k, o[0] - 1],
             device_id=at(o),
             device_id_type=MESH,
         )
 
-    def chip_start(k, value):
+    def goes(a, forward):
+        return t + a < tms if forward else t + a >= tms
+
+    def comes(a, forward):
+        return t >= a if forward else t < a
+
+    steps = sorted(range(1, tms), key=lambda a: -min(a, tms - a))
+
+    def chip_start(k, value, forward):
         mine[k] = value
         pair = partner_copy(k)
         pair.start()
@@ -312,15 +321,31 @@
         first = jnp.where(f == 2, pltpu.roll(value, 64, 1)[0:1], pltpu.roll(value, 96, 1)[1:2])
         both = jnp.where(f == 0, whole[0:1], whole[1:2])
         chip_brief[k] = jnp.where(f < 2, both, first)
+        for a in steps:
+
+            @pl.when(goes(a, forward))
+            def _(a=a):
+                for o in chips:
+                    if o[0] == a:
+                        chip_copy(k, o).start()
+
         for o in chips:
-            chip_copy(k, o).start()
+            if o[0] == 0:
+                chip_copy(k, o).start()
         pair.wait_send()
 
-    def chip_end(k):
+    def chip_end(k, forward):
+        arrived[...] = jnp.zeros(arrived.shape, F32)
         await_all(near_in.at[k], near_recv.at[k])
         own = chip_mine[k] + jnp.sum(near_in[k], axis=0)
-        await_all(far_in.at[k], far_recv.at[k])
-        return own, [jnp.sum(far_in[k, a], axis=0) for a in range(tms - 1)]
+        for a in reversed(steps):
+
+            @pl.when(comes(a, forward))
+            def _(a=a):
+                await_all(far_in.at[k, a - 1], far_recv.at[k, a - 1])
+                arrived[a - 1] = jnp.sum(far_in[k, a - 1], axis=0)
+
+        return own, [arrived[a] for a in range(tms - 1)]
 
     def widen(x):
         f = frame_of_lane((1, 128))
@@ -328,10 +353,8 @@
         return over_frames(jnp.concatenate(rows, axis=0))
 
     def forward_end(k, layer):
-        own, got = chip_end(k)
-        earlier = jnp.zeros((1, 128), F32)
-        for j in range(tms - 1):
-            earlier = earlier + jnp.where(t >= j + 1, got[j], 0.0)
+        own, got = chip_end(k, True)
+        earlier = sum(got[1:], got[0])
         own = moments(widen(earlier) + running(own), counts(t * F))
         ends[layer, 0:1] = own[0]
         ends[layer, 1:2] = own[1]
@@ -346,12 +369,9 @@
         return jnp.concatenate([first, second], axis=0)
 
     def backward_end(k):
-        own, got = chip_end(k)
-        near = jnp.where(t < tms - 1, got[-1], 0.0)
-        later = near
-        for j in range(tms - 2):
-            later = later + jnp.where(t < j + 1, got[j], 0.0)
-        later = widen(later)
+        own, got = chip_end(k, False)
+        near = got[-1]
+        later = widen(sum(got[1:], got[0]))
         f = frame_of_lane((1, 128))
         first = jnp.concatenate([pltpu.roll(near, 96, 1), pltpu.roll(near, 64, 1)], axis=0)
         behind = later - jnp.where(f == 1, first, 0.0)
@@ -402,7 +422,7 @@
             place = (int(down < 0), int(over < 0))
             moves.append(((0, down, over), src, cornerhalo.at[k, 0, place[0], place[1]]))
             moves.append(((turn, down, over), src, cornerhalo.at[k, 1, place[0], place[1]]))
-        return [
+        copies = [
             pltpu.make_async_remote_copy(
                 src_ref=src,
                 dst_ref=dst,
@@ -413,9 +433,24 @@
             )
             for j, (o, src, dst) in enumerate(moves)
         ]
-
-    def side_columns(ks, own, halo, turn, change):
-        inner = F - 2 if turn > 0 else 0
+        packed = [j >= len(PIECES) + 4 for j in range(len(moves))]
+        far = [o[0] != 0 for o, _, _ in moves]
+        pick = lambda p, a: [x for x, y, z in zip(copies, packed, far) if y == p and z == a]
+        return pick(False, False), pick(False, True), pick(True, False), pick(True, True)
+
+    def start_all(*groups):
+        for group in groups:
+            for copy in group:
+                copy.start()
+
+    def await_rims(*groups):
+        for group in groups:
+            for copy in group:
+                copy.wait_recv()
+
+    def side_columns(ks, first, count, turn, change):
+        other = int(count < F)
+        skip = F - 2 if other and turn > 0 else 0
         for side in range(2):
 
             def one(f, carry, side=side):
@@ -423,24 +458,21 @@
                 colside[side, f, pl.ds(1, H)] = change(f, *values)
                 return carry
 
-            lax.fori_loop(0, F + 2, one, 0)
+            lax.fori_loop(first, first + count, one, 0)
             for end, place in ((0, 0), (1, H + 1)):
-                for f in range(F):
-                    values = [cornerhalo[k, 0, end, side, pl.ds(f, 1)] for k in ks]
-                    colside[side, own + f, pl.ds(place, 1)] = change(own + f, *values)
-                for f in range(2):
-                    values = [cornerhalo[k, 1, end, side, pl.ds(inner + f, 1)] for k in ks]
-                    colside[side, halo + f, pl.ds(place, 1)] = change(halo + f, *values)
+                for f in range(count):
+                    values = [cornerhalo[k, other, end, side, pl.ds(skip + f, 1)] for k in ks]
+                    colside[side, first + f, pl.ds(place, 1)] = change(first + f, *values)
 
         @pl.when(c == 0)
         def _():
-            colside[0] = jnp.zeros(colside.shape[1:], F32)
+            colside[0, pl.ds(first, count)] = jnp.zeros((count,) + colside.shape[2:], F32)
 
         @pl.when(c == cols - 1)
         def _():
-            colside[1] = jnp.zeros(colside.shape[1:], F32)
-
-    def build(full, halo, edge, change):
+            colside[1, pl.ds(first, count)] = jnp.zeros((count,) + colside.shape[2:], F32)
+
+    def build(full, first, count, edge, change):
         column = lax.broadcasted_iota(jnp.int32, (6, W, C), 1)
 
         def one(f, carry):
@@ -457,21 +489,23 @@
                 ).astype(BF16)
             return carry
 
-        lax.fori_loop(0, F + 2, one, 0)
+        lax.fori_loop(first, first + count, one, 0)
 
         @pl.when(r == 0)
         def _():
-            taps[:, :, 0] = jnp.zeros((3, F + 2, W, C), BF16)
+            taps[:, pl.ds(first, count), 0] = jnp.zeros((3, count, W, C), BF16)
 
         @pl.when(r == rows - 1)
         def _():
-            taps[:, :, H + 1] = jnp.zeros((3, F + 2, W, C), BF16)
-
-        @pl.when(t == edge)
-        def _():
-            for f in range(2):
-                for dw in range(3):
-                    taps[dw, halo + f] = jnp.zeros((H + 2, W, C), BF16)
+            taps[:, pl.ds(first, count), H + 1] = jnp.zeros((3, count, W, C), BF16)
+
+        if count < F:
+
+            @pl.when(t == edge)
+            def _():
+                for f in range(count):
+                    for dw in range(3):
+                        taps[dw, first + f] = jnp.zeros((H + 2, W, C), BF16)
 
     def convolve(f, weights, back):
         left = jnp.concatenate(
@@ -518,23 +552,18 @@
     pl.semaphore_wait(barrier, len(everyone))
     plane_start(0)
     past = rim_copies(0, actf, 2, 0, 1)
-    for copy in past[1:6]:
-        copy.start()
+    start_all(past[0], past[1][1:])
     pack_rims(0)
-    for copy in past[6:]:
-        copy.start()
+    start_all(past[2], past[3])
     loads[1].wait()
     fill_stage(cotf)
     pack_rims(1)
     line_start(0, plane_end(0))
-    past[0].start()
+    start_all(past[1][:1])
     future = rim_copies(1, cotf, 0, 4, -1)
-    for copy in future:
-        copy.start()
+    start_all(future[0], future[2])
     stat1[...] = first_end()
-
-    for copy in past:
-        copy.wait_recv()
+    start_all(future[1], future[3])
 
     def activate(f, x):
         shape = (1,) * (x.ndim - 1) + (C,)
@@ -543,12 +572,19 @@
         u = (x - mean) * inverse * gain1.reshape(shape) + offset1.reshape(shape)
         return u * sigmoid(u)
 
-    side_columns((0,), 2, 0, 1, activate)
-    build(actf, 0, 0, activate)
+    await_rims(past[0], past[2])
+    side_columns((0,), 2, F, 1, activate)
+    build(actf, 2, F, 0, activate)
     loads[2].wait()
 
     def first_layer(i, carry):
-        f = 2 * i
+        @pl.when(i == 1)
+        def _():
+            await_rims(past[1], past[3])
+            side_columns((0,), 0, 2, 1, activate)
+            build(actf, 0, 2, 0, activate)
+
+        f = 2 - 2 * i
         hidden = convolve(f, w1, False)
         x = actf[pl.ds(f + 2, 2), pl.ds(1, H)].astype(F32).reshape(2 * H * W, C)
         y = (x + hidden + bias1).astype(BF16)
@@ -561,27 +597,31 @@
         return carry
 
     lax.fori_loop(0, F // 2, first_layer, 0)
-    chip_start(1, packed_sums())
+    chip_start(1, packed_sums(), True)
     layer_rims = rim_copies(2, layf, 0, 4, -1)
-    for copy in layer_rims[:6]:
-        copy.start()
+    start_all(layer_rims[0], layer_rims[1])
     fill_stage(layf)
     pack_rims(2)
-    for copy in layer_rims[6:]:
-        copy.start()
-
-    for copy in future:
-        copy.wait_recv()
+    start_all(layer_rims[2], layer_rims[3])
+
+    await_rims(future[0], future[2])
     loads[3].wait()
     same = lambda f, x: x
-    side_columns((1,), 0, 4, -1, same)
-    build(cotf, 4, tms - 1, same)
-
-    def second_grad(f):
+    side_columns((1,), 0, F, -1, same)
+    build(cotf, 0, F, tms - 1, same)
+
+    def second_grad(i, carry):
+        @pl.when(i == 1)
+        def _():
+            await_rims(future[1], future[3])
+            side_columns((1,), 4, 2, -1, same)
+            build(cotf, 4, 2, tms - 1, same)
+
+        f = 2 * i
         grad[pl.ds(f, 2)] = convolve(f, w2, True).reshape(2, H, W, C)
-
-    second_grad(0)
-    second_grad(2)
+        return carry
+
+    lax.fori_loop(0, F // 2, second_grad, 0)
     stat2[...] = forward_end(1, 1)
 
     def second_norm(f, carry):
@@ -600,14 +640,12 @@
         return carry
 
     lax.fori_loop(0, F, second_norm, 0)
-    chip_start(2, backward_terms(packed_sums(), 1))
+    chip_start(2, backward_terms(packed_sums(), 1), False)
     x_rims = rim_copies(3, xf, 0, 4, -1)
-    for copy in x_rims[:6]:
-        copy.start()
+    start_all(x_rims[0], x_rims[1])
     fill_stage(xf)
     pack_rims(3)
-    for copy in x_rims[6:]:
-        copy.start()
+    start_all(x_rims[2], x_rims[3])
     rest2[...] = backward_end(2)
 
     def settle(f, x, v):
@@ -623,8 +661,6 @@
         return carry
 
     lax.fori_loop(0, F, middle, 0)
-    for copy in layer_rims + x_rims:
-        copy.wait_recv()
 
     def settle_rows(f, h, n):
         x, v = xf[f, pl.ds(h, n)].astype(F32), layf[f, pl.ds(h, n)].astype(F32)
@@ -640,13 +676,20 @@
             settle_rows(f, h, 6)
         return carry
 
+    await_rims(layer_rims[0], layer_rims[2], x_rims[0], x_rims[2])
     lax.fori_loop(0, F, middle_rows, 0)
-    lax.fori_loop(F, F + 2, middle_frames, 0)
-    side_columns((3, 2), 0, 4, -1, settle)
-
-    build(gmf, 4, tms - 1, same)
+    side_columns((3, 2), 0, F, -1, settle)
+
+    build(gmf, 0, F, tms - 1, same)
 
     def first_grad(i, carry):
+        @pl.when(i == 1)
+        def _():
+            await_rims(layer_rims[1], layer_rims[3], x_rims[1], x_rims[3])
+            lax.fori_loop(F, F + 2, middle_frames, 0)
+            side_columns((3, 2), 4, 2, -1, settle)
+            build(gmf, 4, 2, tms - 1, same)
+
         f = 2 * i
         grad[pl.ds(f, 2)] = convolve(f, w1, True).reshape(2, H, W, C)
         return carry
@@ -667,7 +710,7 @@
         return carry
 
     lax.fori_loop(0, F, first_norm, 0)
-    chip_start(3, backward_terms(packed_sums(), 0))
+    chip_start(3, backward_terms(packed_sums(), 0), False)
     rest1[...] = backward_end(3)
 
     def finish(f, carry):
@@ -683,13 +726,18 @@
 
     lax.fori_loop(0, F, finish, 0)
 
-    for copy in past + future + layer_rims + x_rims:
-        copy.wait_send()
+    for group in past + future + layer_rims + x_rims:
+        for copy in group:
+            copy.wait_send()
     await_all(plane_in.at[0], plane_send.at[0])
     await_all(line_in.at[0], line_send.at[0])
     for k in range(1, 4):
         await_all(near_in.at[k], near_send.at[k])
-        await_all(far_in.at[k], far_send.at[k])
+        for a in steps:
+
+            @pl.when(goes(a, k == 1))
+            def _(a=a, k=k):
+                await_all(far_in.at[k, a - 1], far_send.at[k, a - 1])
 
 
 def solution(mesh):
@@ -748,10 +796,12 @@
                 pltpu.VMEM((4, 2, 128), F32),
                 pltpu.VMEM((4, n_chips - 1, 2, 128), F32),
                 pltpu.VMEM((4, n_line, n_chips, 1, 128), F32),
+                pltpu.VMEM((n_line, 1, 128), F32),
                 pltpu.SemaphoreType.DMA((9,)),
                 pltpu.SemaphoreType.DMA((4, rims)),
                 pltpu.SemaphoreType.DMA((4, rims)),
-                *[pltpu.SemaphoreType.DMA((4,))] * 10,
+                *[pltpu.SemaphoreType.DMA((4,))] * 8,
+                *[pltpu.SemaphoreType.DMA((4, n_line))] * 2,
             ],
             compiler_params=pltpu.CompilerParams(
                 collective_id=0, has_side_effects=True, vmem_limit_bytes=62 << 20

time: 65.5 us -> 63 us (0.962)
  Pallas kernels: 64.6 us -> 62.2 us
    pallas_call x1, Pallas kernels: 64.6 us -> 62.2 us  [step(): pl.pallas_call(functools.partial(kernel, sizes), name='vae_grad', out_sha...]
where the time goes in v4:
time: 63 us
  Pallas kernels  62.2 us (99%)
  local copies, waits for them, and re-layouts  0.8 us (1%)
    pallas_call x1, Pallas kernels, step(): pl.pallas_call(functools.partial(kernel, sizes), name='vae_grad', out_sha...  62.2 us

profile of v4, /device:TPU:1, one launch (start us, length us, event | category | flops | bytes accessed | tf_op | source)
XLA Modules:
  0.0 63.0 jit_solution(9938507978240260354)
XLA Ops:
  0.0 62.2 %vae_grad.1 = bf16[4,16,16,256]{3,2,1,0:T(8,128)(2,1)S(1)} custom-call(bf16[4,16,16,256]{3,2,1,0:T(8,128)(2,1)} %act_hbm.1, bf16[4,16,16,256]{3,2,1,0:T(8,128)(2,1)} %cot_hbm.1, bf16[27,256,256]{2,1,0:T(8,128)(2,1)} %bitcast.2, bf16[27,256,256]{2,1,0:T(8,128)(2,1)} %bitcast.3, f32[256]{0:T(256)} %bias1_hbm.1, f32[256]{0:T(256)} %gain1_hbm.1, ...), custom_call_target="tpu_custom_call" | custom-call | tf_op jit(solution)/shard_map/vae_grad/pallas_call | solution.py:755
  62.2 0.8 %copy.11 = bf16[4,16,16,256]{3,2,1,0:T(8,128)(2,1)} copy(bf16[4,16,16,256]{3,2,1,0:T(8,128)(2,1)S(1)} %vae_grad.1) | data formatting | bytes 1048576

commit v5 on v4

--- a/solution.py
+++ b/solution.py
@@ -14,7 +14,7 @@
 F, H, W, C, G = 4, 16, 16, 256, 32
 TAPS = tuple(itertools.product(range(3), repeat=3))
 AXES = ("tm", "row", "col")
-PIECES = ((1, 6), (7, 10))
+PIECES = ((1, 11), (12, 5))
 
 
 def offsets_of(sizes):
@@ -30,6 +30,7 @@
         for d in (-1, 0, 1)
     ]
     everyone = list(dict.fromkeys(plane + line + rims))
+    everyone.sort(key=lambda o: -sum(min(x, n - x) for x, n in zip(o, sizes)))
     chips = [
         (a, b, d)
         for a in range(tms)
@@ -115,6 +116,7 @@
     grad,
     layf,
     xf,
+    xwide,
     stage,
     colpack,
     cornerpack,
@@ -472,12 +474,12 @@
         def _():
             colside[1, pl.ds(first, count)] = jnp.zeros((count,) + colside.shape[2:], F32)
 
-    def build(full, first, count, edge, change):
+    def build(get, first, count, edge):
         column = lax.broadcasted_iota(jnp.int32, (6, W, C), 1)
 
         def one(f, carry):
             for h in range(0, H + 2, 6):
-                x = change(f, full[f, pl.ds(h, 6)].astype(F32))
+                x = get(f, h)
                 left = colside[0, f, pl.ds(h, 6)].reshape(6, 1, C)
                 right = colside[1, f, pl.ds(h, 6)].reshape(6, 1, C)
                 taps[1, f, pl.ds(h, 6)] = x.astype(BF16)
@@ -574,7 +576,8 @@
 
     await_rims(past[0], past[2])
     side_columns((0,), 2, F, 1, activate)
-    build(actf, 2, F, 0, activate)
+    active_rows = lambda f, h: activate(f, actf[f, pl.ds(h, 6)].astype(F32))
+    build(active_rows, 2, F, 0)
     loads[2].wait()
 
     def first_layer(i, carry):
@@ -582,7 +585,7 @@
         def _():
             await_rims(past[1], past[3])
             side_columns((0,), 0, 2, 1, activate)
-            build(actf, 0, 2, 0, activate)
+            build(active_rows, 0, 2, 0)
 
         f = 2 - 2 * i
         hidden = convolve(f, w1, False)
@@ -608,14 +611,15 @@
     loads[3].wait()
     same = lambda f, x: x
     side_columns((1,), 0, F, -1, same)
-    build(cotf, 0, F, tms - 1, same)
+    cot_rows = lambda f, h: cotf[f, pl.ds(h, 6)].astype(F32)
+    build(cot_rows, 0, F, tms - 1)
 
     def second_grad(i, carry):
         @pl.when(i == 1)
         def _():
             await_rims(future[1], future[3])
             side_columns((1,), 4, 2, -1, same)
-            build(cotf, 4, 2, tms - 1, same)
+            build(cot_rows, 4, 2, tms - 1)
 
         f = 2 * i
         grad[pl.ds(f, 2)] = convolve(f, w2, True).reshape(2, H, W, C)
@@ -632,20 +636,30 @@
             d = grad[f, pl.ds(h, 8)].reshape(8 * W, C)
             e, da, db = norm_grad(v, d, mean, inverse, gain2, offset2)
             x = cotf[f, pl.ds(h + 1, 8)].astype(F32).reshape(8 * W, C) + inverse * e
-            grad[f, pl.ds(h, 8)] = x.reshape(8, W, C)
+            xwide[f, pl.ds(h + 1, 8)] = x.reshape(8, W, C)
             xf[f, pl.ds(h + 1, 8)] = x.astype(BF16).reshape(8, W, C)
             a, b = a + da, b + db
         part[0, f] = a
         part[1, f] = b
         return carry
 
-    lax.fori_loop(0, F, second_norm, 0)
+    lax.fori_loop(0, 2, second_norm, 0)
+    x_rims = rim_copies(3, xf, 0, 4, -1)
+    start_all(x_rims[1][1:])
+    lax.fori_loop(2, F, second_norm, 0)
     chip_start(2, backward_terms(packed_sums(), 1), False)
-    x_rims = rim_copies(3, xf, 0, 4, -1)
-    start_all(x_rims[0], x_rims[1])
+    start_all(x_rims[0], x_rims[1][:1])
     fill_stage(xf)
     pack_rims(3)
     start_all(x_rims[2], x_rims[3])
+    await_rims(layer_rims[0], layer_rims[2], x_rims[0], x_rims[2])
+
+    def widen_rows(f, carry):
+        for h in (0, H + 1):
+            xwide[f, h] = xf[f, h].astype(F32)
+        return carry
+
+    lax.fori_loop(0, F, widen_rows, 0)
     rest2[...] = backward_end(2)
 
     def settle(f, x, v):
@@ -654,73 +668,49 @@
         r2 = row_of(rest2, f + 8).reshape(shape)
         return x + (r1 + 2.0 * v * r2)
 
-    def middle(f, carry):
-        for h in range(0, H, 8):
-            v = layf[f, pl.ds(h + 1, 8)].astype(F32)
-            gmf[f, pl.ds(h + 1, 8)] = settle(f, grad[f, pl.ds(h, 8)], v).astype(BF16)
-        return carry
-
-    lax.fori_loop(0, F, middle, 0)
-
-    def settle_rows(f, h, n):
-        x, v = xf[f, pl.ds(h, n)].astype(F32), layf[f, pl.ds(h, n)].astype(F32)
-        gmf[f, pl.ds(h, n)] = settle(f, x, v).astype(BF16)
-
-    def middle_rows(f, carry):
-        settle_rows(f, 0, 1)
-        settle_rows(f, H + 1, 1)
-        return carry
-
-    def middle_frames(f, carry):
-        for h in range(0, H + 2, 6):
-            settle_rows(f, h, 6)
-        return carry
-
-    await_rims(layer_rims[0], layer_rims[2], x_rims[0], x_rims[2])
-    lax.fori_loop(0, F, middle_rows, 0)
+    def middle_rows(x):
+        def get(f, h):
+            g = settle(f, x[f, pl.ds(h, 6)].astype(F32), layf[f, pl.ds(h, 6)].astype(F32)).astype(BF16)
+            gmf[f, pl.ds(h, 6)] = g
+            return g.astype(F32)
+
+        return get
+
     side_columns((3, 2), 0, F, -1, settle)
-
-    build(gmf, 0, F, tms - 1, same)
+    build(middle_rows(xwide), 0, F, tms - 1)
 
     def first_grad(i, carry):
         @pl.when(i == 1)
         def _():
             await_rims(layer_rims[1], layer_rims[3], x_rims[1], x_rims[3])
-            lax.fori_loop(F, F + 2, middle_frames, 0)
             side_columns((3, 2), 4, 2, -1, settle)
-            build(gmf, 4, 2, tms - 1, same)
-
-        f = 2 * i
-        grad[pl.ds(f, 2)] = convolve(f, w1, True).reshape(2, H, W, C)
+            build(middle_rows(xf), 4, 2, tms - 1)
+
+        both = convolve(2 * i, w1, True)
+        for j in range(2):
+            f = 2 * i + j
+            mean, inverse = row_of(stat1, f + 2), row_of(stat1, f + 10)
+            a = b = jnp.zeros((8, C), F32)
+            for h in range(0, H, 8):
+                v = actf[f + 2, pl.ds(h + 1, 8)].astype(F32).reshape(8 * W, C)
+                d = both[(j * H + h) * W : (j * H + h + 8) * W]
+                e, da, db = norm_grad(v, d, mean, inverse, gain1, offset1)
+                x = gmf[f, pl.ds(h + 1, 8)].astype(F32).reshape(8 * W, C) + inverse * e
+                grad[f, pl.ds(h, 8)] = x.reshape(8, W, C)
+                a, b = a + da, b + db
+            part[0, f] = a
+            part[1, f] = b
         return carry
 
     lax.fori_loop(0, F // 2, first_grad, 0)
-
-    def first_norm(f, carry):
-        mean, inverse = row_of(stat1, f + 2), row_of(stat1, f + 10)
-        a = b = jnp.zeros((8, C), F32)
-        for h in range(0, H, 8):
-            v = actf[f + 2, pl.ds(h + 1, 8)].astype(F32).reshape(8 * W, C)
-            d = grad[f, pl.ds(h, 8)].reshape(8 * W, C)
-            e, da, db = norm_grad(v, d, mean, inverse, gain1, offset1)
-            grad[f, pl.ds(h, 8)] = e.reshape(8, W, C)
-            a, b = a + da, b + db
-        part[0, f] = a
-        part[1, f] = b
-        return carry
-
-    lax.fori_loop(0, F, first_norm, 0)
     chip_start(3, backward_terms(packed_sums(), 0), False)
     rest1[...] = backward_end(3)
 
     def finish(f, carry):
-        inverse = row_of(stat1, f + 10)
         r1, r2 = row_of(rest1, f), row_of(rest1, f + 8)
         for h in range(0, H, 8):
             v = actf[f + 2, pl.ds(h + 1, 8)].astype(F32).reshape(8 * W, C)
-            e = grad[f, pl.ds(h, 8)].reshape(8 * W, C)
-            x = gmf[f, pl.ds(h + 1, 8)].astype(F32).reshape(8 * W, C)
-            y = x + (inverse * e + r1 + 2.0 * v * r2)
+            y = grad[f, pl.ds(h, 8)].reshape(8 * W, C) + (r1 + 2.0 * v * r2)
             out_ref[f, pl.ds(h, 8)] = y.astype(BF16).reshape(8, W, C)
         return carry
 
@@ -773,6 +763,7 @@
                 pltpu.VMEM((F, H, W, C), F32),
                 pltpu.VMEM(full, BF16),
                 pltpu.VMEM(full, BF16),
+                pltpu.VMEM(full, F32),
                 pltpu.VMEM((2, F * H * W, 128), F32),
                 pltpu.VMEM((4, 2, F, H, C), BF16),
                 pltpu.VMEM((4, 2, 2, F, C), F32),

time: 63 us -> 60.7 us (0.963)
  Pallas kernels: 62.2 us -> 59.9 us
    pallas_call x1, Pallas kernels: 62.2 us -> 59.9 us  [step(): pl.pallas_call(functools.partial(kernel, sizes), name='vae_grad', out_sha...]
where the time goes in v5:
time: 60.7 us
  Pallas kernels  59.9 us (99%)
  local copies, waits for them, and re-layouts  0.8 us (1%)
    pallas_call x1, Pallas kernels, step(): pl.pallas_call(functools.partial(kernel, sizes), name='vae_grad', out_sha...  59.9 us

profile of v5, /device:TPU:1, one launch (start us, length us, event | category | flops | bytes accessed | tf_op | source)
XLA Modules:
  0.0 60.7 jit_solution(5726885489673945781)
XLA Ops:
  0.0 59.9 %vae_grad.1 = bf16[4,16,16,256]{3,2,1,0:T(8,128)(2,1)S(1)} custom-call(bf16[4,16,16,256]{3,2,1,0:T(8,128)(2,1)} %act_hbm.1, bf16[4,16,16,256]{3,2,1,0:T(8,128)(2,1)} %cot_hbm.1, bf16[27,256,256]{2,1,0:T(8,128)(2,1)} %bitcast.2, bf16[27,256,256]{2,1,0:T(8,128)(2,1)} %bitcast.3, f32[256]{0:T(256)} %bias1_hbm.1, f32[256]{0:T(256)} %gain1_hbm.1, ...), custom_call_target="tpu_custom_call" | custom-call | tf_op jit(solution)/shard_map/vae_grad/pallas_call | solution.py:745
  59.9 0.8 %copy.11 = bf16[4,16,16,256]{3,2,1,0:T(8,128)(2,1)} copy(bf16[4,16,16,256]{3,2,1,0:T(8,128)(2,1)S(1)} %vae_grad.1) | data formatting | bytes 1048576

commit v6 on v5

--- a/solution.py
+++ b/solution.py
@@ -14,7 +14,7 @@
 F, H, W, C, G = 4, 16, 16, 256, 32
 TAPS = tuple(itertools.product(range(3), repeat=3))
 AXES = ("tm", "row", "col")
-PIECES = ((1, 11), (12, 5))
+PIECES = ((1, 13), (14, 3))
 
 
 def offsets_of(sizes):
@@ -563,9 +563,8 @@
     line_start(0, plane_end(0))
     start_all(past[1][:1])
     future = rim_copies(1, cotf, 0, 4, -1)
-    start_all(future[0], future[2])
+    start_all(future[0], future[2], future[1], future[3])
     stat1[...] = first_end()
-    start_all(future[1], future[3])
 
     def activate(f, x):
         shape = (1,) * (x.ndim - 1) + (C,)
@@ -602,7 +601,7 @@
     lax.fori_loop(0, F // 2, first_layer, 0)
     chip_start(1, packed_sums(), True)
     layer_rims = rim_copies(2, layf, 0, 4, -1)
-    start_all(layer_rims[0], layer_rims[1])
+    start_all(layer_rims[1], layer_rims[0])
     fill_stage(layf)
     pack_rims(2)
     start_all(layer_rims[2], layer_rims[3])
@@ -648,7 +647,7 @@
     start_all(x_rims[1][1:])
     lax.fori_loop(2, F, second_norm, 0)
     chip_start(2, backward_terms(packed_sums(), 1), False)
-    start_all(x_rims[0], x_rims[1][:1])
+    start_all(x_rims[1][:1], x_rims[0])
     fill_stage(xf)
     pack_rims(3)
     start_all(x_rims[2], x_rims[3])

time: 60.7 us -> 60.7 us (level)
  no operation moved by 1% of the time
where the time goes in v6:
time: 60.7 us; the launch traced here: 60.6 us
  Pallas kernels  59.8 us (99%)
  local copies, waits for them, and re-layouts  0.8 us (1%)
    pallas_call x1, Pallas kernels, step(): pl.pallas_call(functools.partial(kernel, sizes), name='vae_grad', out_sha...  59.8 us

profile of v6, /device:TPU:1, one launch (start us, length us, event | category | flops | bytes accessed | tf_op | source)
XLA Modules:
  0.0 60.6 jit_solution(10865744495007888599)
XLA Ops:
  0.0 59.8 %vae_grad.1 = bf16[4,16,16,256]{3,2,1,0:T(8,128)(2,1)S(1)} custom-call(bf16[4,16,16,256]{3,2,1,0:T(8,128)(2,1)} %act_hbm.1, bf16[4,16,16,256]{3,2,1,0:T(8,128)(2,1)} %cot_hbm.1, bf16[27,256,256]{2,1,0:T(8,128)(2,1)} %bitcast.2, bf16[27,256,256]{2,1,0:T(8,128)(2,1)} %bitcast.3, f32[256]{0:T(256)} %bias1_hbm.1, f32[256]{0:T(256)} %gain1_hbm.1, ...), custom_call_target="tpu_custom_call" | custom-call | tf_op jit(solution)/shard_map/vae_grad/pallas_call | solution.py:744
  59.8 0.8 %copy.11 = bf16[4,16,16,256]{3,2,1,0:T(8,128)(2,1)} copy(bf16[4,16,16,256]{3,2,1,0:T(8,128)(2,1)S(1)} %vae_grad.1) | data formatting | bytes 1048576
